TPU v7x, 32 devices: a whole 2x2x4 slice. The times are simulated.
32 devices in a mesh: rve: 8 (over z, y), blk: 4 (over x, core).
Axes of the slice: x: 2, y: 2, z: 4, core: 2. Of those that a mesh axis runs over, the one named last changes fastest.
Arguments:
- strain: bfloat16 [864, 6], P(('rve', 'blk')), may hold values from -6 to 6
- fiber_coeff: bfloat16 [864, 2048], P(('rve', 'blk')), may hold values from 0.049804688 to 0.8984375
- gradients: float32 [12, 864], P(None, ('rve', 'blk')), may hold values from -6 to 6
- volume: float32 [864], P(('rve', 'blk')), may hold values from 0.1 to 1
- corners: int32 [4, 864], P(None, ('rve', 'blk')), may hold values from 0 to 4095, as said below
- rve_worker: int32 [864], P(('rve', 'blk')), may hold values from 0 to 7, as said below
- rve_slot: int32 [864], P(('rve', 'blk')), may hold values from 0 to 80, as said below
- slot_element: int32 [2592], P(('rve', 'blk')), may hold values from -1 to 863, as said below
- state_table: float32 [2592, 3, 2048], P(('rve', 'blk')), may hold values from -6 to 6
- loading: bfloat16 [6, 3, 2048], replicated, may hold values from -6 to 6
- compliance: bfloat16 [2048, 2048], P('rve'), as said below
Outputs:
- new_states: float32 [2592, 3, 2048], P(('rve', 'blk'))
- node_forces: float32 [3, 4096], P(None, ('rve', 'blk'))
- node_blocks: float32 [9, 4096], P(None, ('rve', 'blk'))
Inputs may be any that keep to these rules, and one draw needn't show every extreme that they name: `rve_worker`: counting the elements of one blk index, each worker number holds between 9 and 81 RVEs, the most reached by some worker; the elements of one aligned block of 27 that name one worker number are never more than 11, a count reached in every draw. `rve_slot`: A worker's RVEs fill its slots from 0 upward; no two elements share a worker and slot. `slot_element`: entry (w * 4 + b) * 81 + s holds e exactly when rve_worker[e] = w, (e // 27) % 4 = b and rve_slot[e] = s; every other entry is -1. The corners of elements in aligned block k of 27 elements are nodes k * 128 to (k + 2) * 128 - 1, and in the last block nodes k * 128 to (k + 1) * 128 - 1. `compliance`: Symmetric.
All inputs are finite; a program needn't handle non-finite values.
Results may differ from a plain program's by a relative error of at most 0.0023.
Values may be sent and summed in bfloat16 or wider, within the bound.
A program may use at most 64 MiB of HBM per device.

v0:
```python
import jax
import jax.numpy as jnp
import numpy as np
from jax import lax
from jax.sharding import PartitionSpec as P

ITERS = 3
NODE_DEV = 128


highest = lax.Precision.HIGHEST


def from_behind(block, axis, distance):
    devices = range(lax.axis_size(axis))
    route = [(i - distance, i) for i in devices if i - distance in devices]
    return lax.ppermute(block, axis, route)


def strain_map():
    voigt_map = np.zeros((6, 3, 3), np.float32)
    for voigt_row, first_axis, second_axis in (
        (0, 0, 0),
        (1, 1, 1),
        (2, 2, 2),
        (3, 1, 2),
        (3, 2, 1),
        (4, 0, 2),
        (4, 2, 0),
        (5, 0, 1),
        (5, 1, 0),
    ):
        voigt_map[voigt_row, first_axis, second_axis] = 1.0
    return jnp.asarray(voigt_map)


def micro_solve(strain_rows, coeff_rows, start_rows, loading, network, basis, fixed_part):
    batch_rows = strain_rows.shape[0]
    node_count = network.shape[0]
    mean_scale = 1.0 / (3 * node_count)
    forcing = jnp.dot(
        strain_rows, loading.reshape(6, 3 * node_count), preferred_element_type=jnp.float32
    ).reshape(batch_rows, 3, node_count)
    fiber_wide = coeff_rows[:, None, :].astype(jnp.float32)
    current = start_rows.reshape(batch_rows, 3, node_count)
    for iteration in range(ITERS):
        pressure = (
            (forcing - fiber_wide * jnp.tanh(current))
            .astype(jnp.bfloat16)
            .reshape(batch_rows * 3, node_count)
        )
        current = lax.dot_general(
            pressure, network, (((1,), (1,)), ((), ())), preferred_element_type=jnp.float32
        ).reshape(batch_rows, 3, node_count)
    flat_state = current.reshape(batch_rows, 3 * node_count)
    load_float = loading.reshape(6, 3 * node_count).astype(jnp.float32)
    stress = jnp.dot(flat_state, load_float.T, precision=highest) * mean_scale
    products = (basis[:, None, :] * basis[None, :, :]).reshape(36, 3 * node_count)
    damping = (fiber_wide * (1.0 - jnp.tanh(current) ** 2)).reshape(batch_rows, 3 * node_count)
    tangent = (
        fixed_part.reshape(1, 36) - jnp.dot(damping, products.T, precision=highest)
    ) * mean_scale
    return (flat_state, stress, tangent)


def body(
    strain,
    fiber_coeff,
    gradients,
    volume,
    corners,
    rve_worker,
    rve_slot,
    slot_element,
    state_table,
    loading,
    compliance,
):
    elem_rows = strain.shape[0]
    workers = lax.axis_size("rve")
    columns = lax.axis_size("blk")
    capacity = state_table.shape[0]
    slot_cap = (capacity + workers - 1) // workers
    node_count = compliance.shape[1]
    buffer_rows = workers * slot_cap
    network = lax.all_gather(compliance, "rve", axis=0, tiled=True)
    basis = lax.dot_general(
        loading.reshape(18, node_count),
        network,
        (((1,), (1,)), ((), ())),
        preferred_element_type=jnp.float32,
    ).reshape(6, 3 * node_count)
    fixed_part = jnp.dot(
        loading.reshape(6, 3 * node_count).astype(jnp.float32), basis.T, precision=highest
    )
    earlier = (rve_worker[None, :] == rve_worker[:, None]) & (rve_slot[None, :] < rve_slot[:, None])
    home_pos = rve_worker * slot_cap + jnp.sum(earlier, axis=1)
    occupied = slot_element >= 0
    source_home = jnp.where(occupied, slot_element // elem_rows // columns, -1)
    slot_ids = jnp.arange(capacity)
    before = (source_home[None, :] == source_home[:, None]) & (
        slot_ids[None, :] < slot_ids[:, None]
    )
    work_pos = jnp.where(occupied, source_home * slot_cap + jnp.sum(before, axis=1), buffer_rows)
    fetch_pos = jnp.minimum(work_pos, buffer_rows - 1)
    flat_table = state_table.reshape(capacity, 3 * node_count)
    send_strain = jnp.zeros((buffer_rows, 6), jnp.bfloat16).at[home_pos].set(strain)
    send_coeff = jnp.zeros((buffer_rows, node_count), jnp.bfloat16).at[home_pos].set(fiber_coeff)
    got_strain, got_coeff = (
        lax.all_to_all(
            send_strain.reshape(workers, slot_cap, 6),
            "rve",
            split_axis=0,
            concat_axis=0,
            tiled=True,
        ),
        lax.all_to_all(
            send_coeff.reshape(workers, slot_cap, node_count),
            "rve",
            split_axis=0,
            concat_axis=0,
            tiled=True,
        ),
    )
    slot_strain = jnp.where(occupied[:, None], got_strain.reshape(buffer_rows, 6)[fetch_pos], 0)
    slot_coeff = jnp.where(
        occupied[:, None], got_coeff.reshape(buffer_rows, node_count)[fetch_pos], 0
    )
    finals, slot_stress, slot_tangent = micro_solve(
        slot_strain, slot_coeff, flat_table, loading, network, basis, fixed_part
    )
    new_table = jnp.where(occupied[:, None], finals, flat_table)
    back_stress = (
        jnp.zeros((buffer_rows, 6), jnp.float32).at[work_pos].set(slot_stress, mode="drop")
    )
    back_tangent = (
        jnp.zeros((buffer_rows, 36), jnp.float32).at[work_pos].set(slot_tangent, mode="drop")
    )
    ret_stress, ret_tangent = (
        lax.all_to_all(
            back_stress.reshape(workers, slot_cap, 6),
            "rve",
            split_axis=0,
            concat_axis=0,
            tiled=True,
        ),
        lax.all_to_all(
            back_tangent.reshape(workers, slot_cap, 36),
            "rve",
            split_axis=0,
            concat_axis=0,
            tiled=True,
        ),
    )
    stress = ret_stress.reshape(buffer_rows, 6)[home_pos]
    tangent = ret_tangent.reshape(buffer_rows, 36)[home_pos]
    gradient_rows = gradients.reshape(4, 3, elem_rows)
    bmatrix = jnp.einsum("vac,ich->ivah", strain_map(), gradient_rows, precision=highest)
    corner_force = volume * jnp.einsum("ivah,hv->iah", bmatrix, stress, precision=highest)
    corner_block = volume * jnp.einsum(
        "ivah,hvw,iwbh->iabh", bmatrix, tangent.reshape(elem_rows, 6, 6), bmatrix, precision=highest
    )
    contrib = jnp.concatenate([corner_force, corner_block.reshape(4, 9, elem_rows)], axis=1)
    contrib = jnp.transpose(contrib, (1, 0, 2)).reshape(12, 4 * elem_rows)
    device_rank = lax.axis_index("rve") * columns + lax.axis_index("blk")
    local_node = (corners - device_rank * NODE_DEV).reshape(4 * elem_rows)
    onehot = (local_node[:, None] == jnp.arange(2 * NODE_DEV)[None, :]).astype(jnp.float32)
    assembled = jnp.dot(contrib, onehot, precision=highest)
    own_rows = assembled[:, :NODE_DEV] + from_behind(assembled[:, NODE_DEV:], ("rve", "blk"), 1)
    return (new_table.reshape(capacity, 3, node_count), own_rows[:3], own_rows[3:])


def solution(mesh):
    return jax.shard_map(
        body,
        mesh=mesh,
        in_specs=(
            P(("rve", "blk"), None),
            P(("rve", "blk"), None),
            P(None, ("rve", "blk")),
            P(("rve", "blk")),
            P(None, ("rve", "blk")),
            P(("rve", "blk")),
            P(("rve", "blk")),
            P(("rve", "blk")),
            P(("rve", "blk"), None, None),
            P(),
            P("rve", None),
        ),
        out_specs=(P(("rve", "blk"), None, None), P(None, ("rve", "blk")), P(None, ("rve", "blk"))),
        check_vma=False,
    )
```

profile of v0, /device:TPU:0, one launch (start us, length us, event | category | flops | bytes accessed | tf_op | source)
XLA Modules:
  0.0 234.0 jit_solution(7010237790635879780)
XLA Ops:
  8.7 0.9 convert_reduce_fusion.1
  11.8 7.3 %all-to-all-start = ((bf16[8,11,6]{1,2,0:T(8,128)(2,1)}), bf16[8,11,6]{1,2,0:T(8,128)(2,1)S(1)}, u32[]{:S(2)}, u32[]{:S(2)}) async-start(bf16[8,11,6]{1,2,0:T(8,128)(2,1)} %copy.60), calls=%async_computation | async-start | bytes 32768 | tf_op jit(solution)/shard_map/all_to_all | solution.py:110
  21.3 1.3 scatter_custom_fusion.1
  22.6 0.9 reshape.136
  23.5 2.3 all-to-all-done
  25.8 3.7 %all-to-all-start.1 = ((bf16[8,11,2048]{2,1,0:T(8,128)(2,1)}), bf16[8,11,2048]{2,1,0:T(8,128)(2,1)S(1)}, u32[]{:S(2)}, u32[]{:S(2)}) async-start(bf16[8,11,2048]{2,1,0:T(8,128)(2,1)} %reshape.136), calls=%async_computation.1 | async-start | bytes 1048576 | tf_op jit(solution)/shard_map/all_to_all | solution.py:117
  31.8 27.5 %all-to-all-done.1 = bf16[8,11,2048]{2,1,0:T(8,128)(2,1)S(1)} async-done(((bf16[8,11,2048]{2,1,0:T(8,128)(2,1)}), bf16[8,11,2048]{2,1,0:T(8,128)(2,1)S(1)}, u32[]{:S(2)}, u32[]{:S(2)}) %all-to-all-start.1) | async-done | bytes 360480 | tf_op jit(solution)/shard_map/all_to_all | solution.py:117
  59.5 0.8 gather_fusion.1
  60.4 88.5 %all-gather.2.cloned.1.call-done = bf16[2048,2048]{1,0:T(8,128)(2,1)} async-done(((bf16[256,2048]{1,0:T(8,128)(2,1)}), bf16[2048,2048]{1,0:T(8,128)(2,1)}) %all-gather.2.cloned.1.call-update) | async-done | bytes 8388624 | tf_op jit(solution)/shard_map/all_gather | solution.py:86
  148.9 12.1 %fusion.25 = bf16[81,3,2048]{2,0,1:T(8,128)(2,1)} fusion(f32[81,3,2048]{2,0,1:T(8,128)S(1)} %fusion.44, bf16[2048,2048]{1,0:T(8,128)(2,1)} %all-gather.2.cloned.1.call-done, f32[81,2048]{1,0:T(8,128)S(1)} %select_convert_fusion, f32[81,3,2048]{2,0,1:T(8,128)} %param.20), kind=kOutput, calls=%fused_computation.20 | convolution fusion | flops 4081342464 | bytes 14028800 | tf_op jit(solution)/shard_map/dot_general | solution.py:52
  161.0 2.1 copy.64
  163.1 0.8 reshape.138
  164.0 5.7 %fusion.59 = f32[243,2048]{1,0:T(8,128)S(1)} fusion(bf16[243,2048]{1,0:T(8,128)(2,1)S(1)} %reshape.138, bf16[2048,2048]{1,0:T(8,128)(2,1)} %all-gather.2.cloned.1.call-done), kind=kOutput, calls=%fused_computation.79 | convolution fusion | flops 2038431744 | bytes 11374592 | tf_op jit(solution)/shard_map/dot_general | solution.py:52
  169.7 1.3 copy-done
  171.1 2.1 reshape_reshape.6
  173.1 3.0 %reshape_reshape.5 = f32[81,3,2048]{2,1,0:T(4,128)S(1)} reshape(f32[243,2048]{1,0:T(8,128)} %copy-done) | data formatting | bytes 3981312 | tf_op jit(solution)/shard_map/reshape;reshape | solution.py:55
  176.2 5.7 %fusion.60 = f32[18,2048]{1,0:T(8,128)S(1)} fusion(bf16[18,2048]{1,0:T(8,128)(2,1)S(1)} %copy-done.5, bf16[2048,2048]{1,0:T(8,128)(2,1)} %all-gather.2.cloned.1.call-done), kind=kOutput, calls=%fused_computation.80 | convolution fusion | flops 150994944 | bytes 8609792 | tf_op jit(solution)/shard_map/dot_general | solution.py:87
  181.9 1.1 broadcast_multiply_fusion
  183.5 2.5 %mul.126 = f32[36,6144]{1,0:T(8,128)} reshape(f32[6,6,6144]{2,1,0:T(8,128)} %broadcast_multiply_fusion) | data formatting | bytes 1769472 | tf_op jit(solution)/shard_map/mul | solution.py:58
  186.0 2.7 %convolution_multiply_fusion.1 = f32[81,6]{0,1:T(8,128)S(1)} fusion(f32[81,6144]{1,0:T(8,128)} %reshape_reshape.6, bf16[6,6144]{1,0:T(8,128)(2,1)S(1)} %bitcast.89), kind=kOutput, calls=%fused_computation.33 | convolution fusion | flops 35832296 | bytes 2066328 | tf_op jit(solution)/shard_map/dot_general | solution.py:57
  190.3 3.3 %all-to-all-start.2 = ((f32[8,11,6]{1,2,0:T(8,128)}), f32[8,11,6]{1,2,0:T(8,128)S(1)}, u32[]{:S(2)}, u32[]{:S(2)}) async-start(f32[8,11,6]{1,2,0:T(8,128)} %copy.68), calls=%async_computation.2 | async-start | bytes 65536 | tf_op jit(solution)/shard_map/all_to_all | solution.py:140
  193.7 1.2 fusion.30
  195.0 1.4 copy.73
  196.3 1.1 pad.6
  197.4 1.5 copy.93
  198.9 1.9 fusion.34
  202.4 5.9 %all-to-all-start.3 = ((f32[8,1,396]{2,1,0:T(1,128)}), f32[8,1,396]{2,1,0:T(1,128)S(1)}, u32[]{:S(2)}, u32[]{:S(2)}) async-start(f32[8,1,396]{2,1,0:T(1,128)} %reshape.239), calls=%async_computation.3 | async-start | bytes 32768 | tf_op jit(solution)/shard_map/all_to_all | solution.py:147
  209.6 5.2 %all-to-all-done.3 = f32[8,1,396]{2,1,0:T(1,128)S(1)} async-done(((f32[8,1,396]{2,1,0:T(1,128)}), f32[8,1,396]{2,1,0:T(1,128)S(1)}, u32[]{:S(2)}, u32[]{:S(2)}) %all-to-all-start.3) | async-done | bytes 12704 | tf_op jit(solution)/shard_map/all_to_all | solution.py:147
  217.3 0.8 fusion.33
  218.7 1.3 collective-permute-start
  220.0 3.5 %copy_select_fusion = f32[81,3,2048]{2,1,0:T(4,128)S(1)} fusion(f32[81,3,2048]{2,1,0:T(4,128)S(1)} %reshape_reshape.5, f32[81,3,2048]{2,0,1:T(8,128)} %param.20, pred[81]{0:T(512)(128)(4,1)S(1)} %broadcast_compare_fusion), kind=kLoop, calls=%fused_computation.16 | loop fusion | flops 497664 | bytes 5972049 | tf_op jit(solution)/shard_map/jit(_where)/select_n | solution.py:132
  223.5 2.5 %copy.80 = f32[81,3,2048]{2,0,1:T(8,128)} copy(f32[81,3,2048]{2,1,0:T(4,128)S(1)} %copy_select_fusion) | data formatting | bytes 3981312
  (84 shorter events, 17.6 us)
Async XLA Ops:
  7.2 23.2 %copy-start.9 = (s32[81]{0:T(128)S(1)}, s32[81]{0:T(128)}, u32[]{:S(2)}) copy-start(s32[81]{0:T(128)} %param.19) | copy-start | bytes 976
  7.2 22.4 %copy-start.6 = (f32[12,27]{1,0:T(8,128)S(1)}, f32[12,27]{1,0:T(8,128)}, u32[]{:S(2)}) copy-start(f32[12,27]{1,0:T(8,128)} %param.14) | copy-start | bytes 3892
  7.2 22.4 %copy-start.4 = (bf16[6,3,2048]{2,1,0:T(4,128)(2,1)S(1)}, bf16[6,3,2048]{2,1,0:T(4,128)(2,1)}, u32[]{:S(2)}) copy-start(bf16[6,3,2048]{2,1,0:T(4,128)(2,1)} %param.21) | copy-start | bytes 221188
  7.2 141.7 %all-gather.2.cloned.1.call-start = ((), (), s32[]{:S(2)}) async-start(), calls=%async_computation.4 | async-start | bytes 9437184 | tf_op jit(solution)/shard_map/all_gather | solution.py:86
  11.8 14.0 %all-to-all-start = ((bf16[8,11,6]{1,2,0:T(8,128)(2,1)}), bf16[8,11,6]{1,2,0:T(8,128)(2,1)S(1)}, u32[]{:S(2)}, u32[]{:S(2)}) async-start(bf16[8,11,6]{1,2,0:T(8,128)(2,1)} %copy.60), calls=%async_computation | async-start | bytes 32768 | tf_op jit(solution)/shard_map/all_to_all | solution.py:110
  25.8 33.5 %all-to-all-start.1 = ((bf16[8,11,2048]{2,1,0:T(8,128)(2,1)}), bf16[8,11,2048]{2,1,0:T(8,128)(2,1)S(1)}, u32[]{:S(2)}, u32[]{:S(2)}) async-start(bf16[8,11,2048]{2,1,0:T(8,128)(2,1)} %reshape.136), calls=%async_computation.1 | async-start | bytes 1048576 | tf_op jit(solution)/shard_map/all_to_all | solution.py:117
  60.4 88.5 %copy-start.2 = (f32[81,2048]{1,0:T(8,128)}, f32[81,2048]{1,0:T(8,128)S(1)}, u32[]{:S(2)}) copy-start(f32[81,2048]{1,0:T(8,128)S(1)} %select_convert_fusion) | copy-start | bytes 1990660
  169.7 1.4 copy-start
  173.1 3.0 %copy-start.5 = (bf16[18,2048]{1,0:T(8,128)(2,1)S(1)}, bf16[18,2048]{1,0:T(8,128)(2,1)}, u32[]{:S(2)}) copy-start(bf16[18,2048]{1,0:T(8,128)(2,1)} %reshape.142) | copy-start | bytes 221188
  183.5 10.2 %copy-start.3 = (f32[81,2048]{1,0:T(8,128)S(1)}, f32[81,2048]{1,0:T(8,128)}, u32[]{:S(2)}) copy-start(f32[81,2048]{1,0:T(8,128)} %copy-done.2) | copy-start | bytes 1990660
  190.3 12.0 %all-to-all-start.2 = ((f32[8,11,6]{1,2,0:T(8,128)}), f32[8,11,6]{1,2,0:T(8,128)S(1)}, u32[]{:S(2)}, u32[]{:S(2)}) async-start(f32[8,11,6]{1,2,0:T(8,128)} %copy.68), calls=%async_computation.2 | async-start | bytes 65536 | tf_op jit(solution)/shard_map/all_to_all | solution.py:140
  197.4 1.5 copy-start.1
  198.9 10.3 %copy-start.7 = (f32[6,3,3,1]{0,2,3,1:T(4,128)S(1)}, f32[6,3,3,1]{0,2,3,1:T(4,128)}, u32[]{:S(2)}) copy-start(f32[6,3,3,1]{0,2,3,1:T(4,128)} %constant.72) | copy-start | bytes 652
  198.9 10.5 %copy-start.8 = (f32[27]{0:T(128)S(1)}, f32[27]{0:T(128)}, u32[]{:S(2)}) copy-start(f32[27]{0:T(128)} %param.15) | copy-start | bytes 328
  202.4 12.5 %all-to-all-start.3 = ((f32[8,1,396]{2,1,0:T(1,128)}), f32[8,1,396]{2,1,0:T(1,128)S(1)}, u32[]{:S(2)}, u32[]{:S(2)}) async-start(f32[8,1,396]{2,1,0:T(1,128)} %reshape.239), calls=%async_computation.3 | async-start | bytes 32768 | tf_op jit(solution)/shard_map/all_to_all | solution.py:147
  218.7 7.3 %collective-permute-start = (f32[12,128]{1,0:T(8,128)S(1)}, f32[12,128]{1,0:T(8,128)S(1)}, u32[]{:S(2)}, u32[]{:S(2)}) collective-permute-start(f32[12,128]{1,0:T(8,128)S(1)} %slice.25), channel_id=1, source_target_pairs={{0,1},{1,2},{2,3},{3,4},{4,5},{5,6},{6,7},{7,8},{8,9},{9,10},{10,1... | collective-permute-start | bytes 18440 | tf_op jit(solution)/shard_map/ppermute | solution.py:17
Sparse Core Ops, SparseCore 0:
  10.2 138.7 all-gather.1
where the time goes:
time: 237 us; the launch traced here: 234 us
  waiting for transfers between devices  124 us (52%)
  local copies, waits for them, and re-layouts  32.6 us (14%)
  matrix products  30.6 us (13%)
  starting transfers between devices  21.6 us (9%)
  between operations  14.4 us (6%)
  other arithmetic  10.5 us (4%)
    all_gather x1, waiting for transfers between devices, body(): network = lax.all_gather(compliance, 'rve', axis=0, tiled=True)  88.5 us
    all_to_all x1, waiting for transfers between devices, body(): lax.all_to_all(send_coeff.reshape(workers, slot_cap, node_count), 'rve',...  27.5 us
    dot_general x2, matrix products, micro_solve(): lax.dot_general(pressure, network, (((1,), (1,)), ((), ())), preferred_el...  17.9 us
    unnamed x28, local copies, waits for them, and re-layouts  8.13 us
    all_to_all x1, starting transfers between devices, body(): lax.all_to_all(send_strain.reshape(workers, slot_cap, 6), 'rve', split_ax...  7.28 us
    all_to_all x1, starting transfers between devices, body(): lax.all_to_all(back_tangent.reshape(workers, slot_cap, 36), 'rve', split_...  5.91 us
    dot_general x1, matrix products, body(): lax.dot_general(loading.reshape(18, node_count), network, (((1,), (1,)),...  5.65 us
    all_to_all x1, waiting for transfers between devices, body(): lax.all_to_all(back_tangent.reshape(workers, slot_cap, 36), 'rve', split_...  5.24 us
  transfers between devices with their start and end apart: 6, of which 4 were waited for; matrix products, arithmetic and copies ran while one was open for 12% of the time, Pallas kernels for 0%

commit v1 on v0

--- a/solution.py
+++ b/solution.py
@@ -2,6 +2,8 @@
 import jax.numpy as jnp
 import numpy as np
 from jax import lax
+from jax.experimental import pallas as pl
+from jax.experimental.pallas import tpu as pltpu
 from jax.sharding import PartitionSpec as P
 
 ITERS = 3
@@ -170,9 +172,274 @@
     return (new_table.reshape(capacity, 3, node_count), own_rows[:3], own_rows[3:])
 
 
+ROW = 16
+SLOT_PAD = 88
+LOAD_PAD = 24
+
+
+def to_column(row):
+    count = row.shape[1]
+    grid_row = lax.broadcasted_iota(jnp.int32, (count, count), 0)
+    grid_col = lax.broadcasted_iota(jnp.int32, (count, count), 1)
+    return jnp.sum(jnp.where(grid_row == grid_col, row, 0), axis=1, keepdims=True)
+
+
+def home_positions(worker_row, slot_row):
+    same = to_column(worker_row) == worker_row
+    ahead = to_column(slot_row) < slot_row
+    rank = jnp.sum(jnp.where(same & ahead, 1, 0), axis=0, keepdims=True)
+    return worker_row * ROW + rank
+
+
+def home_onehot(worker_row, slot_row, rows):
+    positions = home_positions(worker_row, slot_row)
+    row_ids = lax.broadcasted_iota(jnp.int32, (rows, positions.shape[1]), 0)
+    return (row_ids == positions).astype(jnp.float32)
+
+
+def work_onehot(source_row, rows):
+    count = source_row.shape[1]
+    slot_ids = lax.broadcasted_iota(jnp.int32, (count, count), 0)
+    later_ids = lax.broadcasted_iota(jnp.int32, (count, count), 1)
+    same = to_column(source_row) == source_row
+    rank = jnp.sum(jnp.where(same & (slot_ids < later_ids), 1, 0), axis=0, keepdims=True)
+    positions = jnp.where(source_row >= 0, source_row * ROW + rank, -1)
+    column = to_column(positions)
+    lanes = lax.broadcasted_iota(jnp.int32, (count, rows), 1)
+    return (lanes == column).astype(jnp.float32)
+
+
+def dot_nt(left, right, **kwargs):
+    return lax.dot_general(
+        left, right, (((1,), (1,)), ((), ())), preferred_element_type=jnp.float32, **kwargs
+    )
+
+
+def dot_tn(left, right, **kwargs):
+    return lax.dot_general(
+        left, right, (((0,), (0,)), ((), ())), preferred_element_type=jnp.float32, **kwargs
+    )
+
+
+def split_wide(values):
+    high = values.astype(jnp.bfloat16)
+    return high, (values - high.astype(jnp.float32)).astype(jnp.bfloat16)
+
+
+def pack_kernel(strain_ref, fiber_ref, worker_ref, slot_ref, send_ref):
+    rows = send_ref.shape[0]
+    nodes = fiber_ref.shape[1]
+    onehot = home_onehot(worker_ref[...], slot_ref[...], rows).astype(jnp.bfloat16)
+    send_ref[:, :nodes] = jnp.dot(
+        onehot, fiber_ref[...], preferred_element_type=jnp.float32
+    ).astype(jnp.bfloat16)
+    send_ref[:, nodes:] = dot_nt(onehot, strain_ref[...]).astype(jnp.bfloat16)
+
+
+def micro_kernel(
+    got_ref, source_ref, state_ref, loading_ref, halves_ref, new_ref, back_ref,
+    dense, forcing, coeff, current, pressure_a, pressure_b
+):
+    workers, block = halves_ref.shape[0], halves_ref.shape[1]
+    nodes = state_ref.shape[2]
+    capacity = state_ref.shape[1]
+    rows = got_ref.shape[0]
+    mean_scale = 1.0 / (3 * nodes)
+    near = workers // 2
+    for owner in range(workers):
+        for step in range(near + 1):
+            other = (owner + step) % workers
+            if step == near and owner >= near:
+                continue
+            tile = halves_ref[owner, :, step * block:(step + 1) * block]
+            dense[owner * block:(owner + 1) * block, other * block:(other + 1) * block] = tile
+            if step:
+                dense[other * block:(other + 1) * block, owner * block:(owner + 1) * block] = tile.T
+    onehot = work_onehot(source_ref[...], rows)
+    onehot = jnp.concatenate(
+        [onehot, jnp.zeros((SLOT_PAD - capacity, rows), jnp.float32)], axis=0
+    )
+    fetch = onehot.astype(jnp.bfloat16)
+    slots = jnp.dot(fetch, got_ref[...], preferred_element_type=jnp.float32)
+    coeff[...] = slots[:, :nodes]
+    strain_rows = slots[:, nodes:nodes + 8].astype(jnp.bfloat16)
+    forcing[0:LOAD_PAD, :] = loading_ref[...].astype(jnp.float32)
+    current[0:LOAD_PAD, :] = jnp.zeros((LOAD_PAD, nodes), jnp.float32)
+    for axis in range(3):
+        start = LOAD_PAD + axis * SLOT_PAD
+        load = forcing[axis * 8:axis * 8 + 8, :].astype(jnp.bfloat16)
+        forcing[start:start + SLOT_PAD, :] = jnp.dot(
+            strain_rows, load, preferred_element_type=jnp.float32
+        )
+        current[start + 80:start + SLOT_PAD, :] = jnp.zeros((SLOT_PAD - 80, nodes), jnp.float32)
+        current[start:start + capacity, :] = state_ref[axis]
+
+    def press(values, lanes):
+        c = coeff[:, lanes]
+        wide = jnp.concatenate([jnp.zeros((LOAD_PAD, c.shape[1]), jnp.float32), c, c, c], axis=0)
+        return (forcing[:, lanes] - wide * jnp.tanh(values)).astype(jnp.bfloat16)
+
+    for tile in range(nodes // block):
+        lanes = slice(tile * block, (tile + 1) * block)
+        pressure_a[:, lanes] = press(current[:, lanes], lanes)
+    for iteration in range(ITERS):
+        reads, writes = (pressure_a, pressure_b) if iteration % 2 == 0 else (pressure_b, pressure_a)
+        for tile in range(nodes // block):
+            lanes = slice(tile * block, (tile + 1) * block)
+            values = jnp.dot(reads[...], dense[:, lanes], preferred_element_type=jnp.float32)
+            if iteration == ITERS - 1:
+                current[:, lanes] = values
+            else:
+                writes[:, lanes] = press(values, lanes)
+
+    occupied = jnp.sum(onehot, axis=1, keepdims=True) > 0.5
+    tangent = jnp.zeros((SLOT_PAD, 96), jnp.float32)
+    tangent_low = jnp.zeros((SLOT_PAD, 48), jnp.float32)
+    stress = jnp.zeros((SLOT_PAD, 8), jnp.float32)
+    fixed = jnp.zeros((8, 8), jnp.float32)
+    for axis in range(3):
+        start = LOAD_PAD + axis * SLOT_PAD
+        final = current[start:start + SLOT_PAD, :]
+        new_ref[axis] = jnp.where(
+            occupied[:capacity], current[start:start + capacity, :], state_ref[axis]
+        )
+        basis = current[axis * 8:axis * 8 + 8, :]
+        load = forcing[axis * 8:axis * 8 + 8, :].astype(jnp.bfloat16)
+        products = jnp.concatenate([basis[k:k + 1, :] * basis for k in range(6)], axis=0)
+        products_high, products_low = split_wide(products)
+        damping = coeff[...] * (1.0 - jnp.tanh(final) ** 2)
+        damping_high, damping_low = split_wide(damping)
+        tangent += dot_nt(damping_high, jnp.concatenate([products_high, products_low], axis=0))
+        tangent_low += dot_nt(damping_low, products_high)
+        final_high, final_low = split_wide(final)
+        stress += dot_nt(final_high, load) + dot_nt(final_low, load)
+        basis_high, basis_low = split_wide(basis)
+        fixed += dot_nt(load, basis_high) + dot_nt(load, basis_low)
+    lane_ids = lax.broadcasted_iota(jnp.int32, (8, 48), 1)
+    row_ids = lax.broadcasted_iota(jnp.int32, (8, 48), 0)
+    spread = jnp.dot(
+        fixed, (lane_ids % 8 == row_ids).astype(jnp.float32), precision=highest,
+        preferred_element_type=jnp.float32,
+    )
+    fixed_row = jnp.sum(jnp.where(lane_ids // 8 == row_ids, spread, 0.0), axis=0, keepdims=True)
+    total = fixed_row - (tangent[:, :48] + tangent[:, 48:] + tangent_low)
+    packed = jnp.concatenate(
+        [total, stress, jnp.zeros((SLOT_PAD, 72), jnp.float32)], axis=1
+    ) * mean_scale
+    back_ref[...] = dot_tn(onehot, packed, precision=highest)
+
+
+def assemble_kernel(ret_ref, worker_ref, slot_ref, gradient_ref, volume_ref, corner_ref, own_ref, next_ref):
+    rows = ret_ref.shape[0]
+    onehot = home_onehot(worker_ref[...], slot_ref[...], rows)
+    values = dot_tn(ret_ref[...], onehot, precision=highest)
+    volume = volume_ref[...]
+    count = volume.shape[1]
+    stress = [values[48 + k:49 + k, :] for k in range(6)]
+    rows_of = [values[k * 8:k * 8 + 8, :] for k in range(6)]
+    node_ids = lax.broadcasted_iota(jnp.int32, (2 * NODE_DEV, count), 0)
+    assembled = jnp.zeros((16, 2 * NODE_DEV), jnp.float32)
+
+    def apply(g, terms):
+        gx, gy, gz = g
+        return (
+            gx * terms[0] + gz * terms[4] + gy * terms[5],
+            gy * terms[1] + gz * terms[3] + gx * terms[5],
+            gz * terms[2] + gy * terms[3] + gx * terms[4],
+        )
+
+    for corner in range(4):
+        g = [gradient_ref[3 * corner + c:3 * corner + c + 1, :] for c in range(3)]
+        lines = [volume * f for f in apply(g, stress)]
+        for u in apply(g, rows_of):
+            lines += [volume * m for m in apply(g, [u[j:j + 1, :] for j in range(6)])]
+        contrib = jnp.concatenate(lines + [jnp.zeros((4, count), jnp.float32)], axis=0)
+        picked = (node_ids == corner_ref[corner:corner + 1, :]).astype(jnp.float32)
+        assembled += dot_nt(contrib, picked, precision=highest)
+    own_ref[...] = assembled[:, :NODE_DEV]
+    next_ref[...] = assembled[:, NODE_DEV:]
+
+
+def half_network(compliance, workers, columns):
+    block, nodes = compliance.shape
+    mine = lax.axis_index("rve")
+    part = block // columns
+    rows = lax.dynamic_slice(compliance, (lax.axis_index("blk") * part, 0), (part, nodes))
+    doubled = jnp.concatenate([rows, rows], axis=1)
+    near = workers // 2
+    half = lax.dynamic_slice(doubled, (0, mine * block), (part, (near + 1) * block))
+    gathered = lax.all_gather(half, ("rve", "blk"), axis=0, tiled=True)
+    return gathered.reshape(workers, block, (near + 1) * block)
+
+
+def tiled_body(
+    strain, fiber_coeff, gradients, volume, corners, rve_worker, rve_slot, slot_element,
+    state_table, loading, compliance,
+):
+    elem_rows = strain.shape[0]
+    workers = lax.axis_size("rve")
+    columns = lax.axis_size("blk")
+    capacity = state_table.shape[0]
+    nodes = compliance.shape[1]
+    block = compliance.shape[0]
+    rows = workers * ROW
+    vmem = pl.BlockSpec(memory_space=pltpu.VMEM)
+    params = pltpu.CompilerParams(vmem_limit_bytes=56 * 2**20)
+    halves = half_network(compliance, workers, columns)
+    worker_row, slot_row = rve_worker[None, :], rve_slot[None, :]
+    strain_lanes = jnp.pad(strain.T, ((0, 122), (0, 0)))
+    send = pl.pallas_call(
+        pack_kernel,
+        out_shape=jax.ShapeDtypeStruct((rows, nodes + 128), jnp.bfloat16),
+        in_specs=[vmem] * 4, out_specs=vmem, compiler_params=params, name="pack",
+    )(strain_lanes, fiber_coeff, worker_row, slot_row)
+    got = lax.all_to_all(
+        send.reshape(workers, ROW, nodes + 128), "rve", split_axis=0, concat_axis=0, tiled=True
+    ).reshape(rows, nodes + 128)
+    source = jnp.where(slot_element >= 0, slot_element // (elem_rows * columns), -1)[None, :]
+    load_rows = jnp.pad(jnp.transpose(loading, (1, 0, 2)), ((0, 0), (0, 2), (0, 0)))
+    load_rows = load_rows.reshape(LOAD_PAD, nodes)
+    total_rows = LOAD_PAD + 3 * SLOT_PAD
+    new_table, back = pl.pallas_call(
+        micro_kernel,
+        out_shape=(
+            jax.ShapeDtypeStruct((3, capacity, nodes), jnp.float32),
+            jax.ShapeDtypeStruct((rows, 128), jnp.float32),
+        ),
+        in_specs=[vmem] * 5, out_specs=(vmem, vmem),
+        scratch_shapes=[
+            pltpu.VMEM((nodes, nodes), jnp.bfloat16),
+            pltpu.VMEM((total_rows, nodes), jnp.float32),
+            pltpu.VMEM((SLOT_PAD, nodes), jnp.float32),
+            pltpu.VMEM((total_rows, nodes), jnp.float32),
+            pltpu.VMEM((total_rows, nodes), jnp.bfloat16),
+            pltpu.VMEM((total_rows, nodes), jnp.bfloat16),
+        ],
+        compiler_params=params, name="micro",
+    )(got, source, jnp.transpose(state_table, (1, 0, 2)), load_rows, halves)
+    ret = lax.all_to_all(
+        back.reshape(workers, ROW, 128), "rve", split_axis=0, concat_axis=0, tiled=True
+    ).reshape(rows, 128)
+    device_rank = lax.axis_index("rve") * columns + lax.axis_index("blk")
+    own, following = pl.pallas_call(
+        assemble_kernel,
+        out_shape=(jax.ShapeDtypeStruct((16, NODE_DEV), jnp.float32),) * 2,
+        in_specs=[vmem] * 6, out_specs=(vmem, vmem), compiler_params=params, name="assemble",
+    )(ret, worker_row, slot_row, gradients, volume[None, :], corners - device_rank * NODE_DEV)
+    own_rows = own + from_behind(following, ("rve", "blk"), 1)
+    return jnp.transpose(new_table, (1, 0, 2)), own_rows[:3], own_rows[3:12]
+
+
 def solution(mesh):
+    def chosen(*args):
+        workers, columns = lax.axis_size("rve"), lax.axis_size("blk")
+        block = args[-1].shape[0]
+        even = workers % 2 == 0 and block % 128 == 0 and block % (16 * columns) == 0
+        few = -(-args[8].shape[0] // workers) <= ROW and args[8].shape[0] <= SLOT_PAD
+        return (tiled_body if even and few else body)(*args)
+
     return jax.shard_map(
-        body,
+        chosen,
         mesh=mesh,
         in_specs=(
             P(("rve", "blk"), None),

time: 237 us -> 124 us (0.52)
  waiting for transfers between devices: 124 us -> 67.9 us
  matrix products: 30.6 us -> 0 us
  local copies, waits for them, and re-layouts: 32.6 us -> 4.98 us
  Pallas kernels: 0 us -> 19.4 us
  starting transfers between devices: 21.6 us -> 13 us
  other arithmetic: 10.5 us -> 2.59 us
    all_gather x1, waiting for transfers between devices: 88.5 us -> 43.1 us  [half_network(): gathered = lax.all_gather(half, ('rve', 'blk'), axis=0, tiled=True)]
    dot_general x11 -> x0, matrix products: 30.6 us -> none  [the longest x2 17.9 us: micro_solve(): lax.dot_general(pressure, network, (((1,), (1,)), ((), ())), preferred_el...]
    pallas_call x0 -> x3, Pallas kernels: none -> 19.4 us  [the longest x1 14.9 us: tiled_body(): pl.pallas_call(micro_kernel, out_shape=(jax.ShapeDtypeStruct((3, capacity...]
    all_to_all x4 -> x2, waiting for transfers between devices: 35 us -> 23.7 us  [the longest x1 17.4 us: tiled_body(): lax.all_to_all(send.reshape(workers, ROW, nodes + 128), 'rve', split_axis...]
    all_to_all x4 -> x2, starting transfers between devices: 20.2 us -> 11.7 us  [the longest x1 7.29 us: tiled_body(): lax.all_to_all(send.reshape(workers, ROW, nodes + 128), 'rve', split_axis...]
    unnamed x28 -> x13, local copies, waits for them, and re-layouts: 8.13 us -> 1.84 us
    select_n x5 -> x0, other arithmetic: 5.56 us -> none  [the longest x1 3.5 us: body(): new_table = jnp.where(occupied[:, None], finals, flat_table)]
    another operation x2 -> x0, local copies, waits for them, and re-layouts: 5.1 us -> none  [micro_solve(): flat_state = current.reshape(batch_rows, 3 * node_count)]
  transfers between devices with their start and end apart: 6 -> 4, of which waited for: 4 -> 4; matrix products, arithmetic and copies ran while one was open for 12% -> 3% of each run, Pallas kernels for 0% -> 2%
where the time goes in v1:
time: 124 us; the launch traced here: 122 us
  waiting for transfers between devices  67.9 us (55%)
  Pallas kernels  19.4 us (16%)
  between operations  14.1 us (11%)
  starting transfers between devices  13 us (10%)
  local copies, waits for them, and re-layouts  4.98 us (4%)
  other arithmetic  2.59 us (2%)
    all_gather x1, waiting for transfers between devices, half_network(): gathered = lax.all_gather(half, ('rve', 'blk'), axis=0, tiled=True)  43.1 us
    all_to_all x1, waiting for transfers between devices, tiled_body(): lax.all_to_all(send.reshape(workers, ROW, nodes + 128), 'rve', split_axis...  17.4 us
    pallas_call x1, Pallas kernels, tiled_body(): pl.pallas_call(micro_kernel, out_shape=(jax.ShapeDtypeStruct((3, capacity...  14.9 us
    all_to_all x1, starting transfers between devices, tiled_body(): lax.all_to_all(send.reshape(workers, ROW, nodes + 128), 'rve', split_axis...  7.29 us
    all_to_all x1, waiting for transfers between devices, tiled_body(): lax.all_to_all(back.reshape(workers, ROW, 128), 'rve', split_axis=0, conc...  6.32 us
    all_to_all x1, starting transfers between devices, tiled_body(): lax.all_to_all(back.reshape(workers, ROW, 128), 'rve', split_axis=0, conc...  4.38 us
  transfers between devices with their start and end apart: 4, of which 4 were waited for; matrix products, arithmetic and copies ran while one was open for 3% of the time, Pallas kernels for 2%

profile of v1, /device:TPU:0, one launch (start us, length us, event | category | flops | bytes accessed | tf_op | source)
XLA Modules:
  0.0 121.9 jit_solution(17320399382337655466)
XLA Ops:
  7.2 0.0 copy-start
  7.2 0.0 copy-start.3
  7.2 0.0 copy-start.5
  7.2 0.0 all-gather.2.cloned.1.call-start
  7.3 1.1 copy-done
  8.4 0.8 fusion
  9.2 0.0 all-gather.2.cloned.1.call-update
  9.2 1.3 %pad.8.strain_ref = bf16[128,27]{1,0:T(8,128)(2,1)} pad(bf16[6,27]{1,0:T(8,128)(2,1)} %bitcast.23, bf16[]{:T(256)} %constant.13.clone.1), padding=0_122x0_0 | pad | bytes 7238 | tf_op jit(solution)/shard_map/jit(_pad)/pad | solution.py:390
  10.5 2.1 %pack.1 = bf16[128,2176]{1,0:T(8,128)(2,1)} custom-call(bf16[128,27]{1,0:T(8,128)(2,1)} %pad.8.strain_ref, bf16[27,2048]{1,0:T(8,128)(2,1)} %fiber_ref.1, s32[1,27]{1,0:T(1,128)} %bitcast.24, s32[1,27]{1,0:T(1,128)} %bitcast.26), custom_call_target="tpu_custom_call" | custom-call | tf_op jit(solution)/shard_map/pack/pallas_call | solution.py:391
  12.6 7.3 %all-to-all-start = ((bf16[8,16,2176]{2,1,0:T(8,128)(2,1)}), bf16[8,16,2176]{2,1,0:T(8,128)(2,1)S(1)}, u32[]{:S(2)}, u32[]{:S(2)}) async-start(bf16[8,16,2176]{2,1,0:T(8,128)(2,1)} %bitcast.18), calls=%async_computation | async-start | bytes 1114112 | tf_op jit(solution)/shard_map/all_to_all | solution.py:396
  19.9 0.0 copy-done.3
  19.9 0.1 copy.15
  20.0 0.0 copy-done.5
  20.0 0.5 fusion.1.source_ref
  20.5 0.7 pad_bitcast_fusion.loading_ref
  21.2 17.4 %all-to-all-done = bf16[8,16,2176]{2,1,0:T(8,128)(2,1)S(1)} async-done(((bf16[8,16,2176]{2,1,0:T(8,128)(2,1)}), bf16[8,16,2176]{2,1,0:T(8,128)(2,1)S(1)}, u32[]{:S(2)}, u32[]{:S(2)}) %all-to-all-start) | async-done | bytes 557088 | tf_op jit(solution)/shard_map/all_to_all | solution.py:396
  38.6 0.0 copy-start.1
  38.6 43.1 %all-gather.2.cloned.1.call-done = bf16[2048,1280]{1,0:T(8,128)(2,1)} async-done(((bf16[64,1280]{1,0:T(8,128)(2,1)}), bf16[2048,1280]{1,0:T(8,128)(2,1)}) %all-gather.2.cloned.1.call-update) | async-done | bytes 5242896 | tf_op jit(solution)/shard_map/all_gather | solution.py:371
  81.7 0.0 copy-done.1
  81.7 0.0 copy-start.4
  81.7 14.9 %micro.1 = (f32[3,81,2048]{2,1,0:T(8,128)}, f32[128,128]{1,0:T(8,128)}) custom-call(bf16[128,2176]{1,0:T(8,128)(2,1)} %bitcast.17, s32[1,81]{1,0:T(1,128)} %fusion.1.source_ref, f32[3,81,2048]{2,1,0:T(8,128)} %bitcast.19, bf16[24,2048]{1,0:T(8,128)(2,1)} %pad_bitcast_fusion.loading_ref, bf16[8,256,1280]{2,1,0:T(8,128)(2,1)} %bitcast.16), custom_call_target="tpu_custom_call" | custom-call | tf_op jit(solution)/shard_map/micro/pallas_call | solution.py:403
  96.6 4.4 %all-to-all-start.1 = ((f32[8,16,128]{2,1,0:T(8,128)}), f32[8,16,128]{2,1,0:T(8,128)S(1)}, u32[]{:S(2)}, u32[]{:S(2)}) async-start(f32[8,16,128]{2,1,0:T(8,128)} %bitcast.22), calls=%async_computation.1 | async-start | bytes 131072 | tf_op jit(solution)/shard_map/all_to_all | solution.py:420
  100.9 0.0 copy-done.4
  100.9 0.6 broadcast_subtract_fusion.corner_ref
  101.5 6.3 %all-to-all-done.1 = f32[8,16,128]{2,1,0:T(8,128)S(1)} async-done(((f32[8,16,128]{2,1,0:T(8,128)}), f32[8,16,128]{2,1,0:T(8,128)S(1)}, u32[]{:S(2)}, u32[]{:S(2)}) %all-to-all-start.1) | async-done | bytes 65568 | tf_op jit(solution)/shard_map/all_to_all | solution.py:420
  107.8 0.6 copy-done.2
  108.5 2.4 %assemble.1 = (f32[16,128]{1,0:T(8,128)}, f32[16,128]{1,0:T(8,128)}) custom-call(f32[128,128]{1,0:T(8,128)} %bitcast.20, s32[1,27]{1,0:T(1,128)} %bitcast.25, s32[1,27]{1,0:T(1,128)} %bitcast.27, f32[12,27]{1,0:T(8,128)} %gradient_ref.1, f32[1,27]{1,0:T(1,128)} %bitcast.28, s32[4,27]{1,0:T(4,128)} %broadcast_subtract_fusion.corner_ref), custom_call_target="tpu_custom_call" | custom-call | tf_op jit(solution)/shard_map/assemble/pallas_call | solution.py:424
  110.9 1.3 %collective-permute-start = (f32[16,128]{1,0:T(8,128)}, f32[16,128]{1,0:T(8,128)S(1)}, u32[]{:S(2)}, u32[]{:S(2)}) collective-permute-start(f32[16,128]{1,0:T(8,128)} %get-tuple-element.10), channel_id=1, source_target_pairs={{0,1},{1,2},{2,3},{3,4},{4,5},{5,6},{6,7},{7,8},{8,9},{9,10},{10,1... | collective-permute-start | bytes 24584 | tf_op jit(solution)/shard_map/ppermute | solution.py:19
  112.1 1.0 collective-permute-done
  113.2 0.7 add.20
  113.9 0.6 slice.9
  114.5 0.6 slice.8
  (2 shorter events, 0.0 us)
Async XLA Ops:
  7.2 1.2 %copy-start = (bf16[256,2048]{1,0:T(8,128)(2,1)S(1)}, bf16[256,2048]{1,0:T(8,128)(2,1)}, u32[]{:S(2)}) copy-start(bf16[256,2048]{1,0:T(8,128)(2,1)} %param.21) | copy-start | bytes 3145732
  7.2 12.7 %copy-start.3 = (bf16[6,3,2048]{2,1,0:T(4,128)(2,1)S(1)}, bf16[6,3,2048]{2,1,0:T(4,128)(2,1)}, u32[]{:S(2)}) copy-start(bf16[6,3,2048]{2,1,0:T(4,128)(2,1)} %param.20) | copy-start | bytes 221188
  7.2 12.8 %copy-start.5 = (s32[81]{0:T(128)S(1)}, s32[81]{0:T(128)}, u32[]{:S(2)}) copy-start(s32[81]{0:T(128)} %param.18) | copy-start | bytes 976
  7.2 74.5 %all-gather.2.cloned.1.call-start = ((), (), s32[]{:S(2)}) async-start(), calls=%async_computation.2 | async-start | bytes 5406720 | tf_op jit(solution)/shard_map/all_gather | solution.py:371
  12.6 26.0 %all-to-all-start = ((bf16[8,16,2176]{2,1,0:T(8,128)(2,1)}), bf16[8,16,2176]{2,1,0:T(8,128)(2,1)S(1)}, u32[]{:S(2)}, u32[]{:S(2)}) async-start(bf16[8,16,2176]{2,1,0:T(8,128)(2,1)} %bitcast.18), calls=%async_computation | async-start | bytes 1114112 | tf_op jit(solution)/shard_map/all_to_all | solution.py:396
  38.6 43.1 %copy-start.1 = (bf16[8,16,2176]{2,1,0:T(8,128)(2,1)}, bf16[8,16,2176]{2,1,0:T(8,128)(2,1)S(1)}, u32[]{:S(2)}) copy-start(bf16[8,16,2176]{2,1,0:T(8,128)(2,1)S(1)} %all-to-all-done) | copy-start | bytes 1671172
  81.7 19.2 %copy-start.4 = (s32[4,27]{1,0:T(4,128)S(1)}, s32[4,27]{1,0:T(4,128)}, u32[]{:S(2)}) copy-start(s32[4,27]{1,0:T(4,128)} %param.15) | copy-start | bytes 1300
  96.6 11.3 %all-to-all-start.1 = ((f32[8,16,128]{2,1,0:T(8,128)}), f32[8,16,128]{2,1,0:T(8,128)S(1)}, u32[]{:S(2)}, u32[]{:S(2)}) async-start(f32[8,16,128]{2,1,0:T(8,128)} %bitcast.22), calls=%async_computation.1 | async-start | bytes 131072 | tf_op jit(solution)/shard_map/all_to_all | solution.py:420
  107.8 0.6 copy-start.2
  110.9 2.3 %collective-permute-start = (f32[16,128]{1,0:T(8,128)}, f32[16,128]{1,0:T(8,128)S(1)}, u32[]{:S(2)}, u32[]{:S(2)}) collective-permute-start(f32[16,128]{1,0:T(8,128)} %get-tuple-element.10), channel_id=1, source_target_pairs={{0,1},{1,2},{2,3},{3,4},{4,5},{5,6},{6,7},{7,8},{8,9},{9,10},{10,1... | collective-permute-start | bytes 24584 | tf_op jit(solution)/shard_map/ppermute | solution.py:19
Sparse Core Ops, SparseCore 0:
  10.9 70.7 all-gather.1

commit v2 on v1

--- a/solution.py
+++ b/solution.py
@@ -226,14 +226,174 @@
     return high, (values - high.astype(jnp.float32)).astype(jnp.bfloat16)
 
 
-def pack_kernel(strain_ref, fiber_ref, worker_ref, slot_ref, send_ref):
-    rows = send_ref.shape[0]
+MESH = pl.DeviceIdType.MESH
+
+
+def greet(targets):
+    barrier = pltpu.get_barrier_semaphore()
+    for device in targets:
+        pl.semaphore_signal(barrier, inc=1, device_id=device, device_id_type=MESH)
+    pl.semaphore_wait(barrier, len(targets))
+
+
+def exchange(send_ref, recv_ref, send_sems, recv_sems, me, workers):
+    copies = []
+    for offset in range(1, workers):
+        peer = lax.rem(me + offset, workers)
+        source = lax.rem(me + workers - offset, workers)
+        sent = pltpu.make_async_remote_copy(
+            src_ref=send_ref.at[pl.ds(pl.multiple_of(peer * ROW, ROW), ROW)],
+            dst_ref=recv_ref.at[pl.ds(pl.multiple_of(me * ROW, ROW), ROW)],
+            send_sem=send_sems.at[peer],
+            recv_sem=recv_sems.at[me],
+            device_id={"rve": peer},
+            device_id_type=MESH,
+        )
+        sent.start()
+        landing = recv_ref.at[pl.ds(pl.multiple_of(source * ROW, ROW), ROW)]
+        arrival = pltpu.make_async_remote_copy(
+            src_ref=landing,
+            dst_ref=landing,
+            send_sem=send_sems.at[peer],
+            recv_sem=recv_sems.at[source],
+            device_id={"rve": peer},
+            device_id_type=MESH,
+        )
+        copies.append((sent, arrival))
+    here = pl.ds(pl.multiple_of(me * ROW, ROW), ROW)
+    recv_ref[here, :] = send_ref[here, :]
+    return copies
+
+
+def gather_kernel(
+    strain_ref, fiber_ref, worker_ref, slot_ref, compliance_ref, got_ref, net_ref,
+    send_buf, net_send, net_recv, coeff_send, coeff_recv
+):
+    workers, block, width = net_ref.shape
+    near = workers // 2
+    quarter = block // 4
+    me = lax.axis_index("rve")
+    lane = lax.axis_index("blk")
+    z, y = me // 2, lax.rem(me, 2)
+    x, core = lane // 2, lax.rem(lane, 2)
+    routes = (
+        {"rve": me + 2},
+        {"rve": me - 2},
+        {"rve": me + 1 - 2 * y},
+        {"blk": lane + 2 - 4 * x},
+        {"blk": lane + 1 - 2 * core},
+    )
+    up, down, across, over, twin = range(5)
+    greet(
+        [{"rve": lax.rem(me + offset, workers)} for offset in range(1, workers)]
+        + [routes[over], routes[twin]]
+    )
+    for step in range(near):
+        column = pl.multiple_of(lax.rem(me + step, workers) * block, block)
+        net_ref[me, :, step * block:(step + 1) * block] = compliance_ref[:, pl.ds(column, block)]
+    far = pl.multiple_of(lax.rem(me + near, workers) * block, block)
+    left = compliance_ref[:, pl.ds(far, block // 2)]
+    lower = compliance_ref[block // 2:, pl.ds(far, block)].T
+    net_ref[me, :, near * block:] = jnp.where(me < near, left, lower)
+
+    def copy(owner, q, route):
+        piece = net_ref.at[owner, pl.ds(pl.multiple_of(q * quarter, quarter), quarter)]
+        return pltpu.make_async_remote_copy(
+            src_ref=piece,
+            dst_ref=piece,
+            send_sem=net_send.at[owner, q, route],
+            recv_sem=net_recv.at[owner, q],
+            device_id=routes[route],
+            device_id_type=MESH,
+        )
+
+    sends = []
+
+    def push(cond, owner, q, route):
+        sends.append((cond, owner, q, route))
+        if cond is True:
+            copy(owner, q, route).start()
+        else:
+            pl.when(cond)(lambda: copy(owner, q, route).start())
+
+    def arrive(cond, owner, q):
+        if cond is True:
+            copy(owner, q, twin).wait_recv()
+        else:
+            pl.when(cond)(lambda: copy(owner, q, twin).wait_recv())
+
+    k, k2 = 2 * core + x, 2 * core + 1 - x
+    has_up, has_down = z < near - 1, z > 0
+    push(has_up, me, k, up)
+    push(has_down, me, k, down)
+    push(True, me, k, across)
+    push(has_up, me, k2, up)
+    push(has_down, me, k2, down)
+    rows = send_buf.shape[0]
     nodes = fiber_ref.shape[1]
     onehot = home_onehot(worker_ref[...], slot_ref[...], rows).astype(jnp.bfloat16)
-    send_ref[:, :nodes] = jnp.dot(
+    send_buf[:, :nodes] = jnp.dot(
         onehot, fiber_ref[...], preferred_element_type=jnp.float32
     ).astype(jnp.bfloat16)
-    send_ref[:, nodes:] = dot_nt(onehot, strain_ref[...]).astype(jnp.bfloat16)
+    send_buf[:, nodes:] = dot_nt(onehot, strain_ref[...]).astype(jnp.bfloat16)
+    copies = exchange(send_buf, got_ref, coeff_send, coeff_recv, me, workers)
+
+    def lines(distance):
+        if distance == 0:
+            return [(True, me, None, None)]
+        return [
+            (z >= distance, me - 2 * distance, up, has_up),
+            (z < near - distance, me + 2 * distance, down, has_down),
+        ]
+
+    def from_across(distance):
+        for has, owner, route, edge in lines(distance):
+            other = owner + 1 - 2 * y
+            arrive(has, other, k)
+            push(has, other, k, over)
+            push(has, other, k, twin)
+
+    def from_over(distance):
+        for has, owner, route, edge in lines(distance):
+            other = owner + 1 - 2 * y
+            arrive(has, other, k2)
+            push(has, other, k2, twin)
+
+    from_across(0)
+    last = near - 1
+    for distance in range(1, near):
+        for has, owner, route, edge in lines(distance):
+            arrive(has, owner, k)
+            if distance < last:
+                push(has & edge, owner, k, route)
+            push(has, owner, k, across)
+            if distance == last:
+                push(has, owner, k, over)
+            push(has, owner, k, twin)
+        if distance < last:
+            for has, owner, route, edge in lines(distance):
+                arrive(has, owner, k2)
+                if distance + 1 < last:
+                    push(has & edge, owner, k2, route)
+                push(has, owner, k2, twin)
+        from_over(distance - 1)
+        from_across(distance)
+    for has, owner, route, edge in lines(last):
+        arrive(has, owner, k2)
+        push(has, owner, k2, twin)
+    from_over(last)
+    for offset in range(1, workers):
+        owner = lax.rem(me + offset, workers)
+        arrive(True, owner, 2 - 2 * core)
+        arrive(True, owner, 3 - 2 * core)
+    for sent, arrival in copies:
+        arrival.wait_recv()
+        sent.wait_send()
+    for cond, owner, q, route in sends:
+        if cond is True:
+            copy(owner, q, route).wait_send()
+        else:
+            pl.when(cond)(lambda: copy(owner, q, route).wait_send())
 
 
 def micro_kernel(
@@ -248,13 +408,15 @@
     near = workers // 2
     for owner in range(workers):
         for step in range(near + 1):
-            other = (owner + step) % workers
-            if step == near and owner >= near:
-                continue
-            tile = halves_ref[owner, :, step * block:(step + 1) * block]
-            dense[owner * block:(owner + 1) * block, other * block:(other + 1) * block] = tile
+            row, column, width = owner * block, (owner + step) % workers * block, block
+            if step == near:
+                width = block // 2
+                if owner >= near:
+                    row, column = column, row + width
+            tile = halves_ref[owner, :, step * block:step * block + width]
+            dense[row:row + block, column:column + width] = tile
             if step:
-                dense[other * block:(other + 1) * block, owner * block:(owner + 1) * block] = tile.T
+                dense[column:column + width, row:row + block] = tile.T
     onehot = work_onehot(source_ref[...], rows)
     onehot = jnp.concatenate(
         [onehot, jnp.zeros((SLOT_PAD - capacity, rows), jnp.float32)], axis=0
@@ -329,8 +491,26 @@
     back_ref[...] = dot_tn(onehot, packed, precision=highest)
 
 
-def assemble_kernel(ret_ref, worker_ref, slot_ref, gradient_ref, volume_ref, corner_ref, own_ref, next_ref):
+def assemble_kernel(
+    back_ref, worker_ref, slot_ref, gradient_ref, volume_ref, corner_ref, own_ref,
+    ret_ref, next_buf, prev_buf, ret_send, ret_recv, shift_sems
+):
     rows = ret_ref.shape[0]
+    workers, columns = lax.axis_size("rve"), lax.axis_size("blk")
+    me, lane = lax.axis_index("rve"), lax.axis_index("blk")
+    rank = me * columns + lane
+    ahead, behind = lax.rem(rank + 1, workers * columns), lax.rem(
+        rank + workers * columns - 1, workers * columns
+    )
+    following = {"rve": ahead // columns, "blk": lax.rem(ahead, columns)}
+    leading = {"rve": behind // columns, "blk": lax.rem(behind, columns)}
+    greet(
+        [{"rve": lax.rem(me + offset, workers)} for offset in range(1, workers)]
+        + [following, leading]
+    )
+    copies = exchange(back_ref, ret_ref, ret_send, ret_recv, me, workers)
+    for sent, arrival in copies:
+        arrival.wait_recv()
     onehot = home_onehot(worker_ref[...], slot_ref[...], rows)
     values = dot_tn(ret_ref[...], onehot, precision=highest)
     volume = volume_ref[...]
@@ -354,22 +534,18 @@
         for u in apply(g, rows_of):
             lines += [volume * m for m in apply(g, [u[j:j + 1, :] for j in range(6)])]
         contrib = jnp.concatenate(lines + [jnp.zeros((4, count), jnp.float32)], axis=0)
-        picked = (node_ids == corner_ref[corner:corner + 1, :]).astype(jnp.float32)
+        picked = (node_ids == corner_ref[corner:corner + 1, :] - rank * NODE_DEV).astype(jnp.float32)
         assembled += dot_nt(contrib, picked, precision=highest)
-    own_ref[...] = assembled[:, :NODE_DEV]
-    next_ref[...] = assembled[:, NODE_DEV:]
-
-
-def half_network(compliance, workers, columns):
-    block, nodes = compliance.shape
-    mine = lax.axis_index("rve")
-    part = block // columns
-    rows = lax.dynamic_slice(compliance, (lax.axis_index("blk") * part, 0), (part, nodes))
-    doubled = jnp.concatenate([rows, rows], axis=1)
-    near = workers // 2
-    half = lax.dynamic_slice(doubled, (0, mine * block), (part, (near + 1) * block))
-    gathered = lax.all_gather(half, ("rve", "blk"), axis=0, tiled=True)
-    return gathered.reshape(workers, block, (near + 1) * block)
+    next_buf[...] = assembled[:, NODE_DEV:]
+    shift = pltpu.make_async_remote_copy(
+        src_ref=next_buf, dst_ref=prev_buf, send_sem=shift_sems.at[0], recv_sem=shift_sems.at[1],
+        device_id=following, device_id_type=MESH,
+    )
+    shift.start()
+    for sent, arrival in copies:
+        sent.wait_send()
+    shift.wait()
+    own_ref[...] = assembled[:, :NODE_DEV] + jnp.where(rank > 0, prev_buf[...], 0.0)
 
 
 def tiled_body(
@@ -385,17 +561,27 @@
     rows = workers * ROW
     vmem = pl.BlockSpec(memory_space=pltpu.VMEM)
     params = pltpu.CompilerParams(vmem_limit_bytes=56 * 2**20)
-    halves = half_network(compliance, workers, columns)
     worker_row, slot_row = rve_worker[None, :], rve_slot[None, :]
     strain_lanes = jnp.pad(strain.T, ((0, 122), (0, 0)))
-    send = pl.pallas_call(
-        pack_kernel,
-        out_shape=jax.ShapeDtypeStruct((rows, nodes + 128), jnp.bfloat16),
-        in_specs=[vmem] * 4, out_specs=vmem, compiler_params=params, name="pack",
-    )(strain_lanes, fiber_coeff, worker_row, slot_row)
-    got = lax.all_to_all(
-        send.reshape(workers, ROW, nodes + 128), "rve", split_axis=0, concat_axis=0, tiled=True
-    ).reshape(rows, nodes + 128)
+    got, halves = pl.pallas_call(
+        gather_kernel,
+        out_shape=(
+            jax.ShapeDtypeStruct((rows, nodes + 128), jnp.bfloat16),
+            jax.ShapeDtypeStruct((workers, block, workers // 2 * block + block // 2), jnp.bfloat16),
+        ),
+        in_specs=[vmem] * 5, out_specs=(vmem, vmem),
+        scratch_shapes=[
+            pltpu.VMEM((rows, nodes + 128), jnp.bfloat16),
+            pltpu.SemaphoreType.DMA((workers, 4, 5)),
+            pltpu.SemaphoreType.DMA((workers, 4)),
+            pltpu.SemaphoreType.DMA((workers,)),
+            pltpu.SemaphoreType.DMA((workers,)),
+        ],
+        compiler_params=pltpu.CompilerParams(
+            vmem_limit_bytes=40 * 2**20, collective_id=0, has_side_effects=True
+        ),
+        name="gather",
+    )(strain_lanes, fiber_coeff, worker_row, slot_row, compliance)
     source = jnp.where(slot_element >= 0, slot_element // (elem_rows * columns), -1)[None, :]
     load_rows = jnp.pad(jnp.transpose(loading, (1, 0, 2)), ((0, 0), (0, 2), (0, 0)))
     load_rows = load_rows.reshape(LOAD_PAD, nodes)
@@ -417,16 +603,23 @@
         ],
         compiler_params=params, name="micro",
     )(got, source, jnp.transpose(state_table, (1, 0, 2)), load_rows, halves)
-    ret = lax.all_to_all(
-        back.reshape(workers, ROW, 128), "rve", split_axis=0, concat_axis=0, tiled=True
-    ).reshape(rows, 128)
-    device_rank = lax.axis_index("rve") * columns + lax.axis_index("blk")
-    own, following = pl.pallas_call(
+    own_rows = pl.pallas_call(
         assemble_kernel,
-        out_shape=(jax.ShapeDtypeStruct((16, NODE_DEV), jnp.float32),) * 2,
-        in_specs=[vmem] * 6, out_specs=(vmem, vmem), compiler_params=params, name="assemble",
-    )(ret, worker_row, slot_row, gradients, volume[None, :], corners - device_rank * NODE_DEV)
-    own_rows = own + from_behind(following, ("rve", "blk"), 1)
+        out_shape=jax.ShapeDtypeStruct((16, NODE_DEV), jnp.float32),
+        in_specs=[vmem] * 6, out_specs=vmem,
+        scratch_shapes=[
+            pltpu.VMEM((rows, 128), jnp.float32),
+            pltpu.VMEM((16, NODE_DEV), jnp.float32),
+            pltpu.VMEM((16, NODE_DEV), jnp.float32),
+            pltpu.SemaphoreType.DMA((workers,)),
+            pltpu.SemaphoreType.DMA((workers,)),
+            pltpu.SemaphoreType.DMA((2,)),
+        ],
+        compiler_params=pltpu.CompilerParams(
+            vmem_limit_bytes=16 * 2**20, collective_id=1, has_side_effects=True
+        ),
+        name="assemble",
+    )(back, worker_row, slot_row, gradients, volume[None, :], corners)
     return jnp.transpose(new_table, (1, 0, 2)), own_rows[:3], own_rows[3:12]
 
 
@@ -434,7 +627,7 @@
     def chosen(*args):
         workers, columns = lax.axis_size("rve"), lax.axis_size("blk")
         block = args[-1].shape[0]
-        even = workers % 2 == 0 and block % 128 == 0 and block % (16 * columns) == 0
+        even = workers == 8 and columns == 4 and block % 256 == 0
         few = -(-args[8].shape[0] // workers) <= ROW and args[8].shape[0] <= SLOT_PAD
         return (tiled_body if even and few else body)(*args)
 

time: 124 us -> 84 us (0.68); the launches traced: 122 us -> 83.7 us
  waiting for transfers between devices: 67.9 us -> 0 us
  Pallas kernels: 19.4 us -> 71.1 us
  between operations: 14.1 us -> 0.71 us
  starting transfers between devices: 13 us -> 0 us
  local copies, waits for them, and re-layouts: 4.98 us -> 10.7 us
  other arithmetic: 2.59 us -> 1.18 us
    pallas_call x2, Pallas kernels: 4.49 us -> 55.9 us  [the longest x1 44.5 us: tiled_body(): pl.pallas_call(gather_kernel, out_shape=(jax.ShapeDtypeStruct((rows, node...]
    all_gather x1 -> x0, waiting for transfers between devices: 43.1 us -> none  [half_network(): gathered = lax.all_gather(half, ('rve', 'blk'), axis=0, tiled=True)]
    all_to_all x2 -> x0, waiting for transfers between devices: 23.7 us -> none  [the longest x1 17.4 us: tiled_body(): lax.all_to_all(send.reshape(workers, ROW, nodes + 128), 'rve', split_axis...]
    all_to_all x2 -> x0, starting transfers between devices: 11.7 us -> none  [the longest x1 7.29 us: tiled_body(): lax.all_to_all(send.reshape(workers, ROW, nodes + 128), 'rve', split_axis...]
    unnamed x13 -> x25, local copies, waits for them, and re-layouts: 1.84 us -> 8.18 us
    ppermute x1 -> x0, starting transfers between devices: 1.28 us -> none  [from_behind(): return lax.ppermute(block, axis, route)]
  transfers between devices with their start and end apart: 4 -> 0, of which waited for: 4 -> 0; matrix products, arithmetic and copies ran while one was open for 3% -> 0% of each run, Pallas kernels for 2% -> 0%
where the time goes in v2:
time: 84 us; the launch traced here: 83.7 us
  Pallas kernels  71.1 us (85%)
  local copies, waits for them, and re-layouts  10.7 us (13%)
  other arithmetic  1.18 us (1%)
    pallas_call x1, Pallas kernels, tiled_body(): pl.pallas_call(gather_kernel, out_shape=(jax.ShapeDtypeStruct((rows, node...  44.5 us
    pallas_call x1, Pallas kernels, tiled_body(): pl.pallas_call(micro_kernel, out_shape=(jax.ShapeDtypeStruct((3, capacity...  15.1 us
    pallas_call x1, Pallas kernels, tiled_body(): pl.pallas_call(assemble_kernel, out_shape=jax.ShapeDtypeStruct((16, NODE_...  11.5 us
    unnamed x25, local copies, waits for them, and re-layouts  8.18 us

profile of v2, /device:TPU:0, one launch (start us, length us, event | category | flops | bytes accessed | tf_op | source)
XLA Modules:
  0.0 83.7 jit_solution(15065558962710974841)
XLA Ops:
  0.6 1.2 %fusion.source_ref = s32[1,81]{1,0:T(1,128)} fusion(s32[81]{0:T(128)} %param.18), kind=kLoop, calls=%fused_computation.3 | loop fusion | flops 810 | bytes 648 | tf_op jit(solution)/shard_map/broadcast_in_dim | solution.py:585
  1.8 0.7 pad.8.strain_ref
  2.5 1.0 %copy.15 = bf16[3,6,2048]{2,1,0:T(8,128)(2,1)S(1)} copy(bf16[3,6,2048]{2,0,1:T(4,128)(2,1)} %bitcast.17) | data formatting | bytes 147456
  3.5 0.7 pad_bitcast_fusion.loading_ref
  4.1 0.0 copy-start.1
  4.1 1.2 %copy-done.1 = bf16[256,2048]{1,0:T(8,128)(2,1)S(1)} copy-done((bf16[256,2048]{1,0:T(8,128)(2,1)S(1)}, bf16[256,2048]{1,0:T(8,128)(2,1)}, u32[]{:S(2)}) %copy-start.1) | copy-done | bytes 1048600
  5.3 0.0 copy-start.3
  5.3 0.9 %copy-done.3 = bf16[27,2048]{1,0:T(8,128)(2,1)S(1)} copy-done((bf16[27,2048]{1,0:T(8,128)(2,1)S(1)}, bf16[27,2048]{1,0:T(8,128)(2,1)}, u32[]{:S(2)}) %copy-start.3) | copy-done | bytes 110616
  6.2 0.0 copy-start.6
  6.2 0.7 copy-done.6
  6.9 0.0 copy-start.8
  6.9 0.7 copy-done.8
  7.6 44.5 %gather.1 = (bf16[128,2176]{1,0:T(8,128)(2,1)S(1)}, bf16[8,256,1152]{2,1,0:T(8,128)(2,1)S(1)}) custom-call(bf16[128,27]{1,0:T(8,128)(2,1)S(1)} %pad.8.strain_ref, bf16[27,2048]{1,0:T(8,128)(2,1)S(1)} %copy-done.3, s32[1,27]{1,0:T(1,128)S(1)} %bitcast.11, s32[1,27]{1,0:T(1,128)S(1)} %bitcast.13, bf16[256,2048]{1,0:T(8,128)(2,1)S(1)} %copy-done.1), custom_call_target="tpu_custom_call" | custom-call | tf_op jit(solution)/shard_map/gather/pallas_call | solution.py:566
  52.0 0.0 copy-start
  52.0 2.1 %copy-done = bf16[8,256,1152]{2,1,0:T(8,128)(2,1)} copy-done((bf16[8,256,1152]{2,1,0:T(8,128)(2,1)}, bf16[8,256,1152]{2,1,0:T(8,128)(2,1)S(1)}, u32[]{:S(2)}) %copy-start) | copy-done | bytes 4718616
  54.2 0.0 copy-start.2
  54.2 0.8 copy-done.2
  55.0 0.0 copy-start.5
  55.0 0.0 copy-start.9
  55.0 0.0 copy-start.10
  55.0 0.0 copy-start.11
  55.0 15.1 %micro.1 = (f32[3,81,2048]{2,1,0:T(8,128)}, f32[128,128]{1,0:T(8,128)}) custom-call(bf16[128,2176]{1,0:T(8,128)(2,1)} %copy-done.2, s32[1,81]{1,0:T(1,128)} %fusion.source_ref, f32[3,81,2048]{2,1,0:T(8,128)} %bitcast.16, bf16[24,2048]{1,0:T(8,128)(2,1)} %pad_bitcast_fusion.loading_ref, bf16[8,256,1152]{2,1,0:T(8,128)(2,1)} %copy-done), custom_call_target="tpu_custom_call" | custom-call | tf_op jit(solution)/shard_map/micro/pallas_call | solution.py:589
  70.1 0.0 copy-done.5
  70.1 0.0 copy-done.7
  70.1 0.0 copy-done.9
  70.2 0.0 copy-done.10
  70.2 0.0 copy-done.11
  70.2 0.0 copy-start.4
  70.2 0.8 copy-done.4
  71.0 11.5 %assemble.1 = f32[16,128]{1,0:T(8,128)S(1)} custom-call(f32[128,128]{1,0:T(8,128)S(1)} %copy-done.4, s32[1,27]{1,0:T(1,128)S(1)} %bitcast.12, s32[1,27]{1,0:T(1,128)S(1)} %bitcast.14, f32[12,27]{1,0:T(8,128)S(1)} %copy-done.5, f32[1,27]{1,0:T(1,128)S(1)} %bitcast.15, s32[4,27]{1,0:T(4,128)S(1)} %copy-done.10), custom_call_target="tpu_custom_call" | custom-call | tf_op jit(solution)/shard_map/assemble/pallas_call | solution.py:606
  82.5 0.6 slice.6
  83.1 0.6 slice.7
  (1 shorter events, 0.0 us)
Async XLA Ops:
  4.1 1.2 %copy-start.1 = (bf16[256,2048]{1,0:T(8,128)(2,1)S(1)}, bf16[256,2048]{1,0:T(8,128)(2,1)}, u32[]{:S(2)}) copy-start(bf16[256,2048]{1,0:T(8,128)(2,1)} %compliance_ref.1) | copy-start | bytes 3145732
  5.3 0.9 %copy-start.3 = (bf16[27,2048]{1,0:T(8,128)(2,1)S(1)}, bf16[27,2048]{1,0:T(8,128)(2,1)}, u32[]{:S(2)}) copy-start(bf16[27,2048]{1,0:T(8,128)(2,1)} %fiber_ref.1) | copy-start | bytes 331780
  6.2 0.7 copy-start.6
  6.9 0.7 copy-start.8
  52.0 2.1 %copy-start = (bf16[8,256,1152]{2,1,0:T(8,128)(2,1)}, bf16[8,256,1152]{2,1,0:T(8,128)(2,1)S(1)}, u32[]{:S(2)}) copy-start(bf16[8,256,1152]{2,1,0:T(8,128)(2,1)S(1)} %get-tuple-element.8.halves_ref) | copy-start | bytes 14155780
  54.2 0.8 copy-start.2
  55.0 15.2 %copy-start.5 = (f32[12,27]{1,0:T(8,128)S(1)}, f32[12,27]{1,0:T(8,128)}, u32[]{:S(2)}) copy-start(f32[12,27]{1,0:T(8,128)} %gradient_ref.1) | copy-start | bytes 3892
  55.0 15.2 %copy-start.7 = (s32[27]{0:T(128)S(1)}, s32[27]{0:T(128)}, u32[]{:S(2)}) copy-start(s32[27]{0:T(128)} %param.16) | copy-start | bytes 328
  55.0 15.2 %copy-start.9 = (s32[27]{0:T(128)S(1)}, s32[27]{0:T(128)}, u32[]{:S(2)}) copy-start(s32[27]{0:T(128)} %param.17) | copy-start | bytes 328
  55.0 15.2 %copy-start.10 = (s32[4,27]{1,0:T(4,128)S(1)}, s32[4,27]{1,0:T(4,128)}, u32[]{:S(2)}) copy-start(s32[4,27]{1,0:T(4,128)} %corner_ref.1) | copy-start | bytes 1300
  55.0 15.2 %copy-start.11 = (f32[27]{0:T(128)S(1)}, f32[27]{0:T(128)}, u32[]{:S(2)}) copy-start(f32[27]{0:T(128)} %param.14) | copy-start | bytes 328
  70.2 0.8 %copy-start.4 = (f32[128,128]{1,0:T(8,128)S(1)}, f32[128,128]{1,0:T(8,128)}, u32[]{:S(2)}) copy-start(f32[128,128]{1,0:T(8,128)} %get-tuple-element.10.back_ref) | copy-start | bytes 196612

commit v3 on v2

--- a/solution.py
+++ b/solution.py
@@ -265,17 +265,32 @@
     return copies
 
 
-def gather_kernel(
-    strain_ref, fiber_ref, worker_ref, slot_ref, compliance_ref, got_ref, net_ref,
-    send_buf, net_send, net_recv, coeff_send, coeff_recv
+def step_kernel(
+    strain_hbm, fiber_hbm, gradient_hbm, volume_hbm, corner_hbm, worker_hbm, slot_hbm, element_hbm,
+    state_hbm, loading_hbm, compliance_hbm, new_hbm, force_ref, block_ref,
+    strain_ref, fiber_ref, gradient_ref, volume_ref, corner_ref, worker_ref, slot_ref, element_ref,
+    state_ref, loading_ref, left_ref, lower_ref, got_ref, net_ref, send_buf,
+    dense, forcing, coeff, current, pressure_a, pressure_b, back_ref, ret_ref, next_buf, prev_buf,
+    load_sems, net_send, net_recv, coeff_send, coeff_recv, ret_send, ret_recv, shift_sems
 ):
     workers, block, width = net_ref.shape
+    columns = lax.axis_size("blk")
     near = workers // 2
     quarter = block // 4
+    nodes = compliance_hbm.shape[1]
+    elem_rows = fiber_hbm.shape[0]
+    capacity = state_hbm.shape[1]
+    rows = send_buf.shape[0]
+    mean_scale = 1.0 / (3 * nodes)
     me = lax.axis_index("rve")
     lane = lax.axis_index("blk")
     z, y = me // 2, lax.rem(me, 2)
     x, core = lane // 2, lax.rem(lane, 2)
+    rank = me * columns + lane
+    ahead = lax.rem(rank + 1, workers * columns)
+    behind = lax.rem(rank + workers * columns - 1, workers * columns)
+    following = {"rve": ahead // columns, "blk": lax.rem(ahead, columns)}
+    leading = {"rve": behind // columns, "blk": lax.rem(behind, columns)}
     routes = (
         {"rve": me + 2},
         {"rve": me - 2},
@@ -284,17 +299,41 @@
         {"blk": lane + 1 - 2 * core},
     )
     up, down, across, over, twin = range(5)
+    far = pl.multiple_of(lax.rem(me + near, workers) * block, block)
+    own_slab = []
+    for step in range(near):
+        column = pl.multiple_of(lax.rem(me + step, workers) * block, block)
+        own_slab.append((
+            compliance_hbm.at[:, pl.ds(column, block)],
+            net_ref.at[me, :, pl.ds(step * block, block)],
+        ))
+    own_slab += [
+        (compliance_hbm.at[:, pl.ds(far, block // 2)], left_ref),
+        (compliance_hbm.at[pl.ds(block // 2, block // 2), pl.ds(far, block)], lower_ref),
+    ]
+    packs = [
+        (strain_hbm, strain_ref), (fiber_hbm, fiber_ref), (worker_hbm, worker_ref),
+        (slot_hbm, slot_ref),
+    ]
+    laters = [
+        (element_hbm, element_ref), (loading_hbm, loading_ref), (state_hbm, state_ref),
+        (gradient_hbm, gradient_ref), (volume_hbm, volume_ref), (corner_hbm, corner_ref),
+    ]
+    loads = [
+        pltpu.make_async_copy(src, dst, load_sems.at[at])
+        for at, (src, dst) in enumerate(own_slab + packs + laters)
+    ]
+    for load in loads:
+        load.start()
+    slab_loads, pack_loads = loads[:len(own_slab)], loads[len(own_slab):len(own_slab) + len(packs)]
+    later_loads = loads[len(own_slab) + len(packs):]
     greet(
         [{"rve": lax.rem(me + offset, workers)} for offset in range(1, workers)]
-        + [routes[over], routes[twin]]
-    )
-    for step in range(near):
-        column = pl.multiple_of(lax.rem(me + step, workers) * block, block)
-        net_ref[me, :, step * block:(step + 1) * block] = compliance_ref[:, pl.ds(column, block)]
-    far = pl.multiple_of(lax.rem(me + near, workers) * block, block)
-    left = compliance_ref[:, pl.ds(far, block // 2)]
-    lower = compliance_ref[block // 2:, pl.ds(far, block)].T
-    net_ref[me, :, near * block:] = jnp.where(me < near, left, lower)
+        + [routes[over], routes[twin], following, leading]
+    )
+    for load in slab_loads:
+        load.wait()
+    net_ref[me, :, near * block:] = jnp.where(me < near, left_ref[...], lower_ref[...].T)
 
     def copy(owner, q, route):
         piece = net_ref.at[owner, pl.ds(pl.multiple_of(q * quarter, quarter), quarter)]
@@ -329,13 +368,15 @@
     push(True, me, k, across)
     push(has_up, me, k2, up)
     push(has_down, me, k2, down)
-    rows = send_buf.shape[0]
-    nodes = fiber_ref.shape[1]
-    onehot = home_onehot(worker_ref[...], slot_ref[...], rows).astype(jnp.bfloat16)
+    for load in pack_loads:
+        load.wait()
+    home = home_onehot(worker_ref[...], slot_ref[...], rows)
+    home_bf16 = home.astype(jnp.bfloat16)
     send_buf[:, :nodes] = jnp.dot(
-        onehot, fiber_ref[...], preferred_element_type=jnp.float32
+        home_bf16, fiber_ref[...], preferred_element_type=jnp.float32
     ).astype(jnp.bfloat16)
-    send_buf[:, nodes:] = dot_nt(onehot, strain_ref[...]).astype(jnp.bfloat16)
+    send_buf[:, nodes:] = jnp.zeros((rows, 128), jnp.bfloat16)
+    send_buf[:, nodes:nodes + 6] = dot_nt(home_bf16, strain_ref[...]).astype(jnp.bfloat16)
     copies = exchange(send_buf, got_ref, coeff_send, coeff_recv, me, workers)
 
     def lines(distance):
@@ -359,91 +400,113 @@
             arrive(has, other, k2)
             push(has, other, k2, twin)
 
+    def place(owner):
+        rows_here = pl.ds(pl.multiple_of(owner * block, block), block)
+        for step in range(near):
+            there = pl.ds(pl.multiple_of(lax.rem(owner + step, workers) * block, block), block)
+            tile = net_ref[owner, :, step * block:(step + 1) * block]
+            dense[rows_here, there] = tile
+            if step:
+                dense[there, rows_here] = tile.T
+        tile = net_ref[owner, :, near * block:]
+        low = owner < near
+        row = pl.multiple_of(jnp.where(low, owner, owner - near) * block, block)
+        half = block // 2
+        column = pl.multiple_of(jnp.where(low, (owner + near) * block, owner * block + half), half)
+        dense[pl.ds(row, block), pl.ds(column, half)] = tile
+        dense[pl.ds(column, half), pl.ds(row, block)] = tile.T
+
+    def finish(z_other, y_other):
+        owner = z_other * 2 + y_other
+        arrive(True, owner, 2 - 2 * core)
+        arrive(True, owner, 3 - 2 * core)
+        place(owner)
+
+    def setup():
+        for load in later_loads:
+            load.wait()
+        for sent, arrival in copies:
+            arrival.wait_recv()
+        element_row = element_ref[...]
+        source = jnp.full(element_row.shape, -1, jnp.int32)
+        for worker in range(workers):
+            source += jnp.where(element_row >= worker * elem_rows * columns, 1, 0)
+        onehot = work_onehot(source, rows)
+        onehot = jnp.concatenate(
+            [onehot, jnp.zeros((SLOT_PAD - capacity, rows), jnp.float32)], axis=0
+        )
+        slots = jnp.dot(
+            onehot.astype(jnp.bfloat16), got_ref[...], preferred_element_type=jnp.float32
+        )
+        coeff[...] = slots[:, :nodes]
+        strain_rows = slots[:, nodes:nodes + 8].astype(jnp.bfloat16)
+        forcing[0:LOAD_PAD, :] = jnp.zeros((LOAD_PAD, nodes), jnp.float32)
+        for k_load in range(6):
+            three = loading_ref[k_load].astype(jnp.float32)
+            for axis in range(3):
+                forcing[axis * 8 + k_load:axis * 8 + k_load + 1, :] = three[axis:axis + 1, :]
+        current[0:LOAD_PAD, :] = jnp.zeros((LOAD_PAD, nodes), jnp.float32)
+        for axis in range(3):
+            start = LOAD_PAD + axis * SLOT_PAD
+            load_rows = forcing[axis * 8:axis * 8 + 8, :].astype(jnp.bfloat16)
+            forcing[start:start + SLOT_PAD, :] = jnp.dot(
+                strain_rows, load_rows, preferred_element_type=jnp.float32
+            )
+            current[start + 80:start + SLOT_PAD, :] = jnp.zeros((SLOT_PAD - 80, nodes), jnp.float32)
+            current[start:start + capacity, :] = state_ref[axis]
+        for tile in range(nodes // block):
+            lanes = slice(tile * block, (tile + 1) * block)
+            pressure_a[:, lanes] = press(current[:, lanes], lanes)
+        return onehot
+
+    def press(values, lanes):
+        c = coeff[:, lanes]
+        wide = jnp.concatenate([jnp.zeros((LOAD_PAD, c.shape[1]), jnp.float32), c, c, c], axis=0)
+        return (forcing[:, lanes] - wide * jnp.tanh(values)).astype(jnp.bfloat16)
+
+    last = near - 1
+    full = 1
+    z_one = z + 1 - 2 * lax.rem(z, 2)
+    z_two = lax.rem(z + 2, near)
+    z_three = last - z
+
+    def from_over_line(distance):
+        for has, owner, route, edge in lines(distance):
+            arrive(has, owner, k2)
+            push(has, owner, k2, twin)
+
     from_across(0)
-    last = near - 1
+    place(me)
     for distance in range(1, near):
         for has, owner, route, edge in lines(distance):
             arrive(has, owner, k)
             if distance < last:
                 push(has & edge, owner, k, route)
             push(has, owner, k, across)
-            if distance == last:
+            if distance > full:
                 push(has, owner, k, over)
             push(has, owner, k, twin)
-        if distance < last:
+        if distance <= full:
             for has, owner, route, edge in lines(distance):
                 arrive(has, owner, k2)
-                if distance + 1 < last:
+                if distance + 1 <= full:
                     push(has & edge, owner, k2, route)
                 push(has, owner, k2, twin)
         from_over(distance - 1)
+        if distance - 1 > full:
+            from_over_line(distance - 1)
         from_across(distance)
-    for has, owner, route, edge in lines(last):
-        arrive(has, owner, k2)
-        push(has, owner, k2, twin)
+        if distance == 2:
+            finish(z, 1 - y)
+    onehot = setup()
+    finish(z_one, y)
+    from_over_line(last)
     from_over(last)
-    for offset in range(1, workers):
-        owner = lax.rem(me + offset, workers)
-        arrive(True, owner, 2 - 2 * core)
-        arrive(True, owner, 3 - 2 * core)
-    for sent, arrival in copies:
-        arrival.wait_recv()
-        sent.wait_send()
-    for cond, owner, q, route in sends:
-        if cond is True:
-            copy(owner, q, route).wait_send()
-        else:
-            pl.when(cond)(lambda: copy(owner, q, route).wait_send())
-
-
-def micro_kernel(
-    got_ref, source_ref, state_ref, loading_ref, halves_ref, new_ref, back_ref,
-    dense, forcing, coeff, current, pressure_a, pressure_b
-):
-    workers, block = halves_ref.shape[0], halves_ref.shape[1]
-    nodes = state_ref.shape[2]
-    capacity = state_ref.shape[1]
-    rows = got_ref.shape[0]
-    mean_scale = 1.0 / (3 * nodes)
-    near = workers // 2
-    for owner in range(workers):
-        for step in range(near + 1):
-            row, column, width = owner * block, (owner + step) % workers * block, block
-            if step == near:
-                width = block // 2
-                if owner >= near:
-                    row, column = column, row + width
-            tile = halves_ref[owner, :, step * block:step * block + width]
-            dense[row:row + block, column:column + width] = tile
-            if step:
-                dense[column:column + width, row:row + block] = tile.T
-    onehot = work_onehot(source_ref[...], rows)
-    onehot = jnp.concatenate(
-        [onehot, jnp.zeros((SLOT_PAD - capacity, rows), jnp.float32)], axis=0
-    )
-    fetch = onehot.astype(jnp.bfloat16)
-    slots = jnp.dot(fetch, got_ref[...], preferred_element_type=jnp.float32)
-    coeff[...] = slots[:, :nodes]
-    strain_rows = slots[:, nodes:nodes + 8].astype(jnp.bfloat16)
-    forcing[0:LOAD_PAD, :] = loading_ref[...].astype(jnp.float32)
-    current[0:LOAD_PAD, :] = jnp.zeros((LOAD_PAD, nodes), jnp.float32)
-    for axis in range(3):
-        start = LOAD_PAD + axis * SLOT_PAD
-        load = forcing[axis * 8:axis * 8 + 8, :].astype(jnp.bfloat16)
-        forcing[start:start + SLOT_PAD, :] = jnp.dot(
-            strain_rows, load, preferred_element_type=jnp.float32
-        )
-        current[start + 80:start + SLOT_PAD, :] = jnp.zeros((SLOT_PAD - 80, nodes), jnp.float32)
-        current[start:start + capacity, :] = state_ref[axis]
-
-    def press(values, lanes):
-        c = coeff[:, lanes]
-        wide = jnp.concatenate([jnp.zeros((LOAD_PAD, c.shape[1]), jnp.float32), c, c, c], axis=0)
-        return (forcing[:, lanes] - wide * jnp.tanh(values)).astype(jnp.bfloat16)
-
-    for tile in range(nodes // block):
-        lanes = slice(tile * block, (tile + 1) * block)
-        pressure_a[:, lanes] = press(current[:, lanes], lanes)
+    finish(z_one, 1 - y)
+    for z_other in (z_two, z_three):
+        finish(z_other, y)
+        finish(z_other, 1 - y)
+
     for iteration in range(ITERS):
         reads, writes = (pressure_a, pressure_b) if iteration % 2 == 0 else (pressure_b, pressure_a)
         for tile in range(nodes // block):
@@ -462,7 +525,7 @@
     for axis in range(3):
         start = LOAD_PAD + axis * SLOT_PAD
         final = current[start:start + SLOT_PAD, :]
-        new_ref[axis] = jnp.where(
+        state_ref[axis] = jnp.where(
             occupied[:capacity], current[start:start + capacity, :], state_ref[axis]
         )
         basis = current[axis * 8:axis * 8 + 8, :]
@@ -477,6 +540,8 @@
         stress += dot_nt(final_high, load) + dot_nt(final_low, load)
         basis_high, basis_low = split_wide(basis)
         fixed += dot_nt(load, basis_high) + dot_nt(load, basis_low)
+    store = pltpu.make_async_copy(state_ref, new_hbm, load_sems.at[len(loads)])
+    store.start()
     lane_ids = lax.broadcasted_iota(jnp.int32, (8, 48), 1)
     row_ids = lax.broadcasted_iota(jnp.int32, (8, 48), 0)
     spread = jnp.dot(
@@ -489,30 +554,17 @@
         [total, stress, jnp.zeros((SLOT_PAD, 72), jnp.float32)], axis=1
     ) * mean_scale
     back_ref[...] = dot_tn(onehot, packed, precision=highest)
-
-
-def assemble_kernel(
-    back_ref, worker_ref, slot_ref, gradient_ref, volume_ref, corner_ref, own_ref,
-    ret_ref, next_buf, prev_buf, ret_send, ret_recv, shift_sems
-):
-    rows = ret_ref.shape[0]
-    workers, columns = lax.axis_size("rve"), lax.axis_size("blk")
-    me, lane = lax.axis_index("rve"), lax.axis_index("blk")
-    rank = me * columns + lane
-    ahead, behind = lax.rem(rank + 1, workers * columns), lax.rem(
-        rank + workers * columns - 1, workers * columns
-    )
-    following = {"rve": ahead // columns, "blk": lax.rem(ahead, columns)}
-    leading = {"rve": behind // columns, "blk": lax.rem(behind, columns)}
-    greet(
-        [{"rve": lax.rem(me + offset, workers)} for offset in range(1, workers)]
-        + [following, leading]
-    )
-    copies = exchange(back_ref, ret_ref, ret_send, ret_recv, me, workers)
+    returns = exchange(back_ref, ret_ref, ret_send, ret_recv, me, workers)
     for sent, arrival in copies:
+        sent.wait_send()
+    for cond, owner, q, route in sends:
+        if cond is True:
+            copy(owner, q, route).wait_send()
+        else:
+            pl.when(cond)(lambda: copy(owner, q, route).wait_send())
+    for sent, arrival in returns:
         arrival.wait_recv()
-    onehot = home_onehot(worker_ref[...], slot_ref[...], rows)
-    values = dot_tn(ret_ref[...], onehot, precision=highest)
+    values = dot_tn(ret_ref[...], home, precision=highest)
     volume = volume_ref[...]
     count = volume.shape[1]
     stress = [values[48 + k:49 + k, :] for k in range(6)]
@@ -542,10 +594,13 @@
         device_id=following, device_id_type=MESH,
     )
     shift.start()
-    for sent, arrival in copies:
+    for sent, arrival in returns:
         sent.wait_send()
     shift.wait()
-    own_ref[...] = assembled[:, :NODE_DEV] + jnp.where(rank > 0, prev_buf[...], 0.0)
+    own = assembled[:, :NODE_DEV] + jnp.where(rank > 0, prev_buf[...], 0.0)
+    force_ref[...] = own[:3]
+    block_ref[...] = own[3:12]
+    store.wait()
 
 
 def tiled_body(
@@ -554,73 +609,68 @@
 ):
     elem_rows = strain.shape[0]
     workers = lax.axis_size("rve")
-    columns = lax.axis_size("blk")
     capacity = state_table.shape[0]
     nodes = compliance.shape[1]
     block = compliance.shape[0]
     rows = workers * ROW
+    total = LOAD_PAD + 3 * SLOT_PAD
     vmem = pl.BlockSpec(memory_space=pltpu.VMEM)
-    params = pltpu.CompilerParams(vmem_limit_bytes=56 * 2**20)
-    worker_row, slot_row = rve_worker[None, :], rve_slot[None, :]
-    strain_lanes = jnp.pad(strain.T, ((0, 122), (0, 0)))
-    got, halves = pl.pallas_call(
-        gather_kernel,
+    hbm = pl.BlockSpec(memory_space=pl.ANY)
+    wide, narrow, whole = jnp.float32, jnp.bfloat16, jnp.int32
+    dma = pltpu.SemaphoreType.DMA
+    new_table, forces, blocks = pl.pallas_call(
+        step_kernel,
         out_shape=(
-            jax.ShapeDtypeStruct((rows, nodes + 128), jnp.bfloat16),
-            jax.ShapeDtypeStruct((workers, block, workers // 2 * block + block // 2), jnp.bfloat16),
+            jax.ShapeDtypeStruct((3, capacity, nodes), wide),
+            jax.ShapeDtypeStruct((3, NODE_DEV), wide),
+            jax.ShapeDtypeStruct((9, NODE_DEV), wide),
         ),
-        in_specs=[vmem] * 5, out_specs=(vmem, vmem),
+        in_specs=[hbm] * 11, out_specs=(hbm, vmem, vmem),
         scratch_shapes=[
-            pltpu.VMEM((rows, nodes + 128), jnp.bfloat16),
-            pltpu.SemaphoreType.DMA((workers, 4, 5)),
-            pltpu.SemaphoreType.DMA((workers, 4)),
-            pltpu.SemaphoreType.DMA((workers,)),
-            pltpu.SemaphoreType.DMA((workers,)),
+            pltpu.VMEM((6, elem_rows), narrow),
+            pltpu.VMEM((elem_rows, nodes), narrow),
+            pltpu.VMEM((12, elem_rows), wide),
+            pltpu.VMEM((1, elem_rows), wide),
+            pltpu.VMEM((4, elem_rows), whole),
+            pltpu.VMEM((1, elem_rows), whole),
+            pltpu.VMEM((1, elem_rows), whole),
+            pltpu.VMEM((1, capacity), whole),
+            pltpu.VMEM((3, capacity, nodes), wide),
+            pltpu.VMEM((6, 3, nodes), narrow),
+            pltpu.VMEM((block, block // 2), narrow),
+            pltpu.VMEM((block // 2, block), narrow),
+            pltpu.VMEM((rows, nodes + 128), narrow),
+            pltpu.VMEM((workers, block, workers // 2 * block + block // 2), narrow),
+            pltpu.VMEM((rows, nodes + 128), narrow),
+            pltpu.VMEM((nodes, nodes), narrow),
+            pltpu.VMEM((total, nodes), wide),
+            pltpu.VMEM((SLOT_PAD, nodes), wide),
+            pltpu.VMEM((total, nodes), wide),
+            pltpu.VMEM((total, nodes), narrow),
+            pltpu.VMEM((total, nodes), narrow),
+            pltpu.VMEM((rows, 128), wide),
+            pltpu.VMEM((rows, 128), wide),
+            pltpu.VMEM((16, NODE_DEV), wide),
+            pltpu.VMEM((16, NODE_DEV), wide),
+            dma((workers // 2 + 13,)),
+            dma((workers, 4, 5)),
+            dma((workers, 4)),
+            dma((workers,)),
+            dma((workers,)),
+            dma((workers,)),
+            dma((workers,)),
+            dma((2,)),
         ],
         compiler_params=pltpu.CompilerParams(
-            vmem_limit_bytes=40 * 2**20, collective_id=0, has_side_effects=True
+            vmem_limit_bytes=58 * 2**20, collective_id=0, has_side_effects=True
         ),
-        name="gather",
-    )(strain_lanes, fiber_coeff, worker_row, slot_row, compliance)
-    source = jnp.where(slot_element >= 0, slot_element // (elem_rows * columns), -1)[None, :]
-    load_rows = jnp.pad(jnp.transpose(loading, (1, 0, 2)), ((0, 0), (0, 2), (0, 0)))
-    load_rows = load_rows.reshape(LOAD_PAD, nodes)
-    total_rows = LOAD_PAD + 3 * SLOT_PAD
-    new_table, back = pl.pallas_call(
-        micro_kernel,
-        out_shape=(
-            jax.ShapeDtypeStruct((3, capacity, nodes), jnp.float32),
-            jax.ShapeDtypeStruct((rows, 128), jnp.float32),
-        ),
-        in_specs=[vmem] * 5, out_specs=(vmem, vmem),
-        scratch_shapes=[
-            pltpu.VMEM((nodes, nodes), jnp.bfloat16),
-            pltpu.VMEM((total_rows, nodes), jnp.float32),
-            pltpu.VMEM((SLOT_PAD, nodes), jnp.float32),
-            pltpu.VMEM((total_rows, nodes), jnp.float32),
-            pltpu.VMEM((total_rows, nodes), jnp.bfloat16),
-            pltpu.VMEM((total_rows, nodes), jnp.bfloat16),
-        ],
-        compiler_params=params, name="micro",
-    )(got, source, jnp.transpose(state_table, (1, 0, 2)), load_rows, halves)
-    own_rows = pl.pallas_call(
-        assemble_kernel,
-        out_shape=jax.ShapeDtypeStruct((16, NODE_DEV), jnp.float32),
-        in_specs=[vmem] * 6, out_specs=vmem,
-        scratch_shapes=[
-            pltpu.VMEM((rows, 128), jnp.float32),
-            pltpu.VMEM((16, NODE_DEV), jnp.float32),
-            pltpu.VMEM((16, NODE_DEV), jnp.float32),
-            pltpu.SemaphoreType.DMA((workers,)),
-            pltpu.SemaphoreType.DMA((workers,)),
-            pltpu.SemaphoreType.DMA((2,)),
-        ],
-        compiler_params=pltpu.CompilerParams(
-            vmem_limit_bytes=16 * 2**20, collective_id=1, has_side_effects=True
-        ),
-        name="assemble",
-    )(back, worker_row, slot_row, gradients, volume[None, :], corners)
-    return jnp.transpose(new_table, (1, 0, 2)), own_rows[:3], own_rows[3:12]
+        name="step",
+    )(
+        strain.T, fiber_coeff, gradients, volume[None, :], corners, rve_worker[None, :],
+        rve_slot[None, :], slot_element[None, :], jnp.transpose(state_table, (1, 0, 2)),
+        loading, compliance,
+    )
+    return jnp.transpose(new_table, (1, 0, 2)), forces, blocks
 
 
 def solution(mesh):

time: 84 us -> 69.3 us (0.82)
  Pallas kernels: 71.1 us -> 64.1 us
  local copies, waits for them, and re-layouts: 10.7 us -> 4.38 us
  other arithmetic: 1.18 us -> 0 us
    pallas_call x3 -> x1, Pallas kernels: 71.1 us -> 64.1 us  [tiled_body(): pl.pallas_call(step_kernel, out_shape=(jax.ShapeDtypeStruct((3, capacity,...]
    unnamed x25 -> x7, local copies, waits for them, and re-layouts: 8.18 us -> 4.38 us
    slice x2 -> x0, local copies, waits for them, and re-layouts: 1.18 us -> none  [tiled_body(): return (jnp.transpose(new_table, (1, 0, 2)), own_rows[:3], own_rows[3:12])]
    broadcast_in_dim x1 -> x0, other arithmetic: 1.18 us -> none  [tiled_body(): jnp.where(slot_element >= 0, slot_element // (elem_rows * columns), -1)]
where the time goes in v3:
time: 69.3 us; the launch traced here: 69.1 us
  Pallas kernels  64.1 us (92%)
  local copies, waits for them, and re-layouts  4.38 us (6%)
    pallas_call x1, Pallas kernels, tiled_body(): pl.pallas_call(step_kernel, out_shape=(jax.ShapeDtypeStruct((3, capacity,...  64.1 us
    unnamed x7, local copies, waits for them, and re-layouts  4.38 us

profile of v3, /device:TPU:0, one launch (start us, length us, event | category | flops | bytes accessed | tf_op | source)
XLA Modules:
  0.0 69.1 jit_solution(9067472950973034595)
XLA Ops:
  0.6 64.1 %step.1 = (f32[3,81,2048]{2,1,0:T(8,128)}, f32[3,128]{1,0:T(4,128)}, f32[9,128]{1,0:T(8,128)}) custom-call(bf16[6,27]{1,0:T(8,128)(2,1)} %bitcast.9, bf16[27,2048]{1,0:T(8,128)(2,1)} %fiber_hbm.1, f32[12,27]{1,0:T(8,128)} %gradient_hbm.1, f32[1,27]{1,0:T(1,128)} %bitcast.10, s32[4,27]{1,0:T(4,128)} %corner_hbm.1, s32[1,27]{1,0:T(1,128)} %bitcast.11, ...), custom_call_target="tpu_custom_call" | custom-call | tf_op jit(solution)/shard_map/step/pallas_call | solution.py:621
  64.7 0.0 copy-start.1
  64.7 0.0 copy-start
  64.8 3.2 %copy.17 = f32[81,3,2048]{2,0,1:T(8,128)} copy(f32[81,3,2048]{2,0,1:T(8,128)} %bitcast.8) | data formatting | bytes 3981312
  67.9 0.0 copy-done.1
  68.0 0.6 copy.18
  68.5 0.0 copy-done
  68.5 0.6 copy.19
Async XLA Ops:
  64.7 3.2 %copy-start.1 = (f32[3,128]{1,0:T(4,128)S(1)}, f32[3,128]{1,0:T(4,128)}, u32[]{:S(2)}) copy-start(f32[3,128]{1,0:T(4,128)} %get-tuple-element.13) | copy-start | bytes 4612
  64.7 3.8 %copy-start = (f32[9,128]{1,0:T(8,128)S(1)}, f32[9,128]{1,0:T(8,128)}, u32[]{:S(2)}) copy-start(f32[9,128]{1,0:T(8,128)} %get-tuple-element.14) | copy-start | bytes 13828

commit v4 on v3

--- a/solution.py
+++ b/solution.py
@@ -173,6 +173,7 @@
 
 
 ROW = 16
+PARTS = 2
 SLOT_PAD = 88
 LOAD_PAD = 24
 
@@ -184,29 +185,35 @@
     return jnp.sum(jnp.where(grid_row == grid_col, row, 0), axis=1, keepdims=True)
 
 
-def home_positions(worker_row, slot_row):
+def home_positions(worker_row, slot_row, slots):
     same = to_column(worker_row) == worker_row
     ahead = to_column(slot_row) < slot_row
     rank = jnp.sum(jnp.where(same & ahead, 1, 0), axis=0, keepdims=True)
-    return worker_row * ROW + rank
+    return worker_row * slots + rank
 
 
 def home_onehot(worker_row, slot_row, rows):
-    positions = home_positions(worker_row, slot_row)
+    positions = home_positions(worker_row, slot_row, ROW)
     row_ids = lax.broadcasted_iota(jnp.int32, (rows, positions.shape[1]), 0)
     return (row_ids == positions).astype(jnp.float32)
 
 
-def work_onehot(source_row, rows):
+def work_positions(source_row, slots):
     count = source_row.shape[1]
     slot_ids = lax.broadcasted_iota(jnp.int32, (count, count), 0)
     later_ids = lax.broadcasted_iota(jnp.int32, (count, count), 1)
     same = to_column(source_row) == source_row
     rank = jnp.sum(jnp.where(same & (slot_ids < later_ids), 1, 0), axis=0, keepdims=True)
-    positions = jnp.where(source_row >= 0, source_row * ROW + rank, -1)
-    column = to_column(positions)
-    lanes = lax.broadcasted_iota(jnp.int32, (count, rows), 1)
-    return (lanes == column).astype(jnp.float32)
+    shifted = jnp.where(source_row >= 0, source_row * slots + rank + 2, 0)
+    grid_row = lax.broadcasted_iota(jnp.int32, (SLOT_PAD, count), 0)
+    grid_col = lax.broadcasted_iota(jnp.int32, (SLOT_PAD, count), 1)
+    return jnp.sum(jnp.where(grid_row == grid_col, shifted, 0), axis=1, keepdims=True) - 2
+
+
+def folded_positions(row_ids, fold, tile, slots):
+    inside = fold * ROW + (row_ids & (ROW - 1)) - tile * slots
+    target = (row_ids >> 4) * slots + inside
+    return jnp.where((inside >= 0) & (inside < slots), target, -1)
 
 
 def dot_nt(left, right, **kwargs):
@@ -276,7 +283,7 @@
     workers, block, width = net_ref.shape
     columns = lax.axis_size("blk")
     near = workers // 2
-    quarter = block // 4
+    piece_rows = block // (4 * PARTS)
     nodes = compliance_hbm.shape[1]
     elem_rows = fiber_hbm.shape[0]
     capacity = state_hbm.shape[1]
@@ -336,7 +343,7 @@
     net_ref[me, :, near * block:] = jnp.where(me < near, left_ref[...], lower_ref[...].T)
 
     def copy(owner, q, route):
-        piece = net_ref.at[owner, pl.ds(pl.multiple_of(q * quarter, quarter), quarter)]
+        piece = net_ref.at[owner, pl.ds(pl.multiple_of(q * piece_rows, piece_rows), piece_rows)]
         return pltpu.make_async_remote_copy(
             src_ref=piece,
             dst_ref=piece,
@@ -363,20 +370,38 @@
 
     k, k2 = 2 * core + x, 2 * core + 1 - x
     has_up, has_down = z < near - 1, z > 0
-    push(has_up, me, k, up)
-    push(has_down, me, k, down)
-    push(True, me, k, across)
-    push(has_up, me, k2, up)
-    push(has_down, me, k2, down)
+    def parts(q):
+        return [q * PARTS + part for part in range(PARTS)]
+
+    for q in parts(k):
+        push(has_up, me, q, up)
+        push(has_down, me, q, down)
+        push(True, me, q, across)
+    for q in parts(k2):
+        push(has_up, me, q, up)
+        push(has_down, me, q, down)
     for load in pack_loads:
         load.wait()
     home = home_onehot(worker_ref[...], slot_ref[...], rows)
-    home_bf16 = home.astype(jnp.bfloat16)
-    send_buf[:, :nodes] = jnp.dot(
-        home_bf16, fiber_ref[...], preferred_element_type=jnp.float32
-    ).astype(jnp.bfloat16)
-    send_buf[:, nodes:] = jnp.zeros((rows, 128), jnp.bfloat16)
-    send_buf[:, nodes:nodes + 6] = dot_nt(home_bf16, strain_ref[...]).astype(jnp.bfloat16)
+    slots_each = (capacity + workers - 1) // workers
+    tiles = nodes // 128 + 1
+    home_at = home_positions(worker_ref[...], slot_ref[...], slots_each)
+    row_ids = lax.broadcasted_iota(jnp.int32, (rows, elem_rows), 0)
+    for fold in range(send_buf.shape[1] // 128):
+        packed = jnp.zeros((rows, 128), jnp.float32)
+        for tile in range(fold * ROW // slots_each, (fold * ROW + ROW - 1) // slots_each + 1):
+            target = folded_positions(row_ids, fold, tile, slots_each)
+            picked = (target == home_at).astype(jnp.bfloat16)
+            if tile < tiles - 1:
+                packed += jnp.dot(
+                    picked, fiber_ref[:, tile * 128:(tile + 1) * 128],
+                    preferred_element_type=jnp.float32,
+                )
+            elif tile == tiles - 1:
+                packed += jnp.concatenate(
+                    [dot_nt(picked, strain_ref[...]), jnp.zeros((rows, 122), jnp.float32)], axis=1
+                )
+        send_buf[:, fold * 128:(fold + 1) * 128] = packed.astype(jnp.bfloat16)
     copies = exchange(send_buf, got_ref, coeff_send, coeff_recv, me, workers)
 
     def lines(distance):
@@ -390,15 +415,17 @@
     def from_across(distance):
         for has, owner, route, edge in lines(distance):
             other = owner + 1 - 2 * y
-            arrive(has, other, k)
-            push(has, other, k, over)
-            push(has, other, k, twin)
+            for q in parts(k):
+                arrive(has, other, q)
+                push(has, other, q, over)
+                push(has, other, q, twin)
 
     def from_over(distance):
         for has, owner, route, edge in lines(distance):
             other = owner + 1 - 2 * y
-            arrive(has, other, k2)
-            push(has, other, k2, twin)
+            for q in parts(k2):
+                arrive(has, other, q)
+                push(has, other, q, twin)
 
     def place(owner):
         rows_here = pl.ds(pl.multiple_of(owner * block, block), block)
@@ -418,8 +445,8 @@
 
     def finish(z_other, y_other):
         owner = z_other * 2 + y_other
-        arrive(True, owner, 2 - 2 * core)
-        arrive(True, owner, 3 - 2 * core)
+        for q in parts(2 - 2 * core) + parts(3 - 2 * core):
+            arrive(True, owner, q)
         place(owner)
 
     def setup():
@@ -431,15 +458,22 @@
         source = jnp.full(element_row.shape, -1, jnp.int32)
         for worker in range(workers):
             source += jnp.where(element_row >= worker * elem_rows * columns, 1, 0)
-        onehot = work_onehot(source, rows)
-        onehot = jnp.concatenate(
-            [onehot, jnp.zeros((SLOT_PAD - capacity, rows), jnp.float32)], axis=0
-        )
-        slots = jnp.dot(
-            onehot.astype(jnp.bfloat16), got_ref[...], preferred_element_type=jnp.float32
-        )
-        coeff[...] = slots[:, :nodes]
-        strain_rows = slots[:, nodes:nodes + 8].astype(jnp.bfloat16)
+        lane_at = lax.broadcasted_iota(jnp.int32, (SLOT_PAD, rows), 1)
+        onehot = (lane_at == work_positions(source, ROW)).astype(jnp.float32)
+        work_at = work_positions(source, slots_each)
+        for tile in range(tiles):
+            wanted = jnp.zeros((SLOT_PAD, 128), jnp.float32)
+            first, final = tile * slots_each // ROW, (tile * slots_each + slots_each - 1) // ROW
+            for fold in range(first, final + 1):
+                target = folded_positions(lane_at, fold, tile, slots_each)
+                wanted += jnp.dot(
+                    (target == work_at).astype(jnp.bfloat16),
+                    got_ref[:, fold * 128:(fold + 1) * 128],
+                    preferred_element_type=jnp.float32,
+                )
+            if tile < tiles - 1:
+                coeff[:, tile * 128:(tile + 1) * 128] = wanted
+        strain_rows = wanted[:, :8].astype(jnp.bfloat16)
         forcing[0:LOAD_PAD, :] = jnp.zeros((LOAD_PAD, nodes), jnp.float32)
         for k_load in range(6):
             three = loading_ref[k_load].astype(jnp.float32)
@@ -472,31 +506,34 @@
 
     def from_over_line(distance):
         for has, owner, route, edge in lines(distance):
-            arrive(has, owner, k2)
-            push(has, owner, k2, twin)
+            for q in parts(k2):
+                arrive(has, owner, q)
+                push(has, owner, q, twin)
 
     from_across(0)
-    place(me)
     for distance in range(1, near):
         for has, owner, route, edge in lines(distance):
-            arrive(has, owner, k)
-            if distance < last:
-                push(has & edge, owner, k, route)
-            push(has, owner, k, across)
-            if distance > full:
-                push(has, owner, k, over)
-            push(has, owner, k, twin)
+            for q in parts(k):
+                arrive(has, owner, q)
+                if distance < last:
+                    push(has & edge, owner, q, route)
+                push(has, owner, q, across)
+                if distance > full:
+                    push(has, owner, q, over)
+                push(has, owner, q, twin)
         if distance <= full:
             for has, owner, route, edge in lines(distance):
-                arrive(has, owner, k2)
-                if distance + 1 <= full:
-                    push(has & edge, owner, k2, route)
-                push(has, owner, k2, twin)
+                for q in parts(k2):
+                    arrive(has, owner, q)
+                    if distance + 1 <= full:
+                        push(has & edge, owner, q, route)
+                    push(has, owner, q, twin)
         from_over(distance - 1)
         if distance - 1 > full:
             from_over_line(distance - 1)
         from_across(distance)
         if distance == 2:
+            place(me)
             finish(z, 1 - y)
     onehot = setup()
     finish(z_one, y)
@@ -614,6 +651,8 @@
     block = compliance.shape[0]
     rows = workers * ROW
     total = LOAD_PAD + 3 * SLOT_PAD
+    slots_each = (capacity + workers - 1) // workers
+    folded = ((nodes // 128 + 1) * slots_each + ROW - 1) // ROW
     vmem = pl.BlockSpec(memory_space=pltpu.VMEM)
     hbm = pl.BlockSpec(memory_space=pl.ANY)
     wide, narrow, whole = jnp.float32, jnp.bfloat16, jnp.int32
@@ -639,9 +678,9 @@
             pltpu.VMEM((6, 3, nodes), narrow),
             pltpu.VMEM((block, block // 2), narrow),
             pltpu.VMEM((block // 2, block), narrow),
-            pltpu.VMEM((rows, nodes + 128), narrow),
+            pltpu.VMEM((rows, folded * 128), narrow),
             pltpu.VMEM((workers, block, workers // 2 * block + block // 2), narrow),
-            pltpu.VMEM((rows, nodes + 128), narrow),
+            pltpu.VMEM((rows, folded * 128), narrow),
             pltpu.VMEM((nodes, nodes), narrow),
             pltpu.VMEM((total, nodes), wide),
             pltpu.VMEM((SLOT_PAD, nodes), wide),
@@ -653,8 +692,8 @@
             pltpu.VMEM((16, NODE_DEV), wide),
             pltpu.VMEM((16, NODE_DEV), wide),
             dma((workers // 2 + 13,)),
-            dma((workers, 4, 5)),
-            dma((workers, 4)),
+            dma((workers, 4 * PARTS, 5)),
+            dma((workers, 4 * PARTS)),
             dma((workers,)),
             dma((workers,)),
             dma((workers,)),

time: 69.3 us -> 65.4 us (0.944)
  Pallas kernels: 64.1 us -> 60.2 us
    pallas_call x1, Pallas kernels: 64.1 us -> 60.2 us  [tiled_body(): pl.pallas_call(step_kernel, out_shape=(jax.ShapeDtypeStruct((3, capacity,...]
where the time goes in v4:
time: 65.4 us; the launch traced here: 65.2 us
  Pallas kernels  60.2 us (92%)
  local copies, waits for them, and re-layouts  4.38 us (7%)
  between operations  0.66 us (1%)
    pallas_call x1, Pallas kernels, tiled_body(): pl.pallas_call(step_kernel, out_shape=(jax.ShapeDtypeStruct((3, capacity,...  60.2 us
    unnamed x7, local copies, waits for them, and re-layouts  4.38 us

profile of v4, /device:TPU:0, one launch (start us, length us, event | category | flops | bytes accessed | tf_op | source)
XLA Modules:
  0.0 65.2 jit_solution(10566197558899976844)
XLA Ops:
  0.6 60.2 %step.1 = (f32[3,81,2048]{2,1,0:T(8,128)}, f32[3,128]{1,0:T(4,128)}, f32[9,128]{1,0:T(8,128)}) custom-call(bf16[6,27]{1,0:T(8,128)(2,1)} %bitcast.9, bf16[27,2048]{1,0:T(8,128)(2,1)} %fiber_hbm.1, f32[12,27]{1,0:T(8,128)} %gradient_hbm.1, f32[1,27]{1,0:T(1,128)} %bitcast.10, s32[4,27]{1,0:T(4,128)} %corner_hbm.1, s32[1,27]{1,0:T(1,128)} %bitcast.11, ...), custom_call_target="tpu_custom_call" | custom-call | tf_op jit(solution)/shard_map/step/pallas_call | solution.py:660
  60.8 0.0 copy-start.1
  60.8 0.0 copy-start
  60.9 3.2 %copy.17 = f32[81,3,2048]{2,0,1:T(8,128)} copy(f32[81,3,2048]{2,0,1:T(8,128)} %bitcast.8) | data formatting | bytes 3981312
  64.1 0.0 copy-done.1
  64.1 0.6 copy.18
  64.6 0.0 copy-done
  64.6 0.6 copy.19
Async XLA Ops:
  60.8 3.2 %copy-start.1 = (f32[3,128]{1,0:T(4,128)S(1)}, f32[3,128]{1,0:T(4,128)}, u32[]{:S(2)}) copy-start(f32[3,128]{1,0:T(4,128)} %get-tuple-element.13) | copy-start | bytes 4612
  60.8 3.8 %copy-start = (f32[9,128]{1,0:T(8,128)S(1)}, f32[9,128]{1,0:T(8,128)}, u32[]{:S(2)}) copy-start(f32[9,128]{1,0:T(8,128)} %get-tuple-element.14) | copy-start | bytes 13828

commit v5 on v4

--- a/solution.py
+++ b/solution.py
@@ -274,7 +274,7 @@
 
 def step_kernel(
     strain_hbm, fiber_hbm, gradient_hbm, volume_hbm, corner_hbm, worker_hbm, slot_hbm, element_hbm,
-    state_hbm, loading_hbm, compliance_hbm, new_hbm, force_ref, block_ref,
+    state_hbm, loading_hbm, compliance_hbm, new_hbm, own_ref,
     strain_ref, fiber_ref, gradient_ref, volume_ref, corner_ref, worker_ref, slot_ref, element_ref,
     state_ref, loading_ref, left_ref, lower_ref, got_ref, net_ref, send_buf,
     dense, forcing, coeff, current, pressure_a, pressure_b, back_ref, ret_ref, next_buf, prev_buf,
@@ -538,11 +538,12 @@
     onehot = setup()
     finish(z_one, y)
     from_over_line(last)
+    finish(z_one, 1 - y)
+    finish(z_two, y)
     from_over(last)
-    finish(z_one, 1 - y)
-    for z_other in (z_two, z_three):
-        finish(z_other, y)
-        finish(z_other, 1 - y)
+    finish(z_three, y)
+    finish(z_two, 1 - y)
+    finish(z_three, 1 - y)
 
     for iteration in range(ITERS):
         reads, writes = (pressure_a, pressure_b) if iteration % 2 == 0 else (pressure_b, pressure_a)
@@ -634,10 +635,34 @@
     for sent, arrival in returns:
         sent.wait_send()
     shift.wait()
-    own = assembled[:, :NODE_DEV] + jnp.where(rank > 0, prev_buf[...], 0.0)
-    force_ref[...] = own[:3]
-    block_ref[...] = own[3:12]
+    own_ref[...] = assembled[:, :NODE_DEV] + jnp.where(rank > 0, prev_buf[...], 0.0)
     store.wait()
+
+
+def deliver_kernel(solved_hbm, own_ref, new_hbm, force_ref, block_ref, held, in_sems, out_sems):
+    width = solved_hbm.shape[2] // 4
+    chunks = [(axis, cut) for axis in range(3) for cut in range(4)]
+
+    def part(ref, axis, cut):
+        return ref.at[axis, :, pl.ds(cut * width, width)]
+
+    arriving = [
+        pltpu.make_async_copy(part(solved_hbm, *at), part(held, *at), in_sems.at[at])
+        for at in chunks
+    ]
+    leaving = [
+        pltpu.make_async_copy(part(held, *at), part(new_hbm, *at), out_sems.at[at])
+        for at in chunks
+    ]
+    for copy in arriving:
+        copy.start()
+    force_ref[...] = own_ref[0:3, :]
+    block_ref[...] = own_ref[3:12, :]
+    for came, goes in zip(arriving, leaving):
+        came.wait()
+        goes.start()
+    for copy in leaving:
+        copy.wait()
 
 
 def tiled_body(
@@ -657,14 +682,13 @@
     hbm = pl.BlockSpec(memory_space=pl.ANY)
     wide, narrow, whole = jnp.float32, jnp.bfloat16, jnp.int32
     dma = pltpu.SemaphoreType.DMA
-    new_table, forces, blocks = pl.pallas_call(
+    solved, own_rows = pl.pallas_call(
         step_kernel,
         out_shape=(
             jax.ShapeDtypeStruct((3, capacity, nodes), wide),
-            jax.ShapeDtypeStruct((3, NODE_DEV), wide),
-            jax.ShapeDtypeStruct((9, NODE_DEV), wide),
+            jax.ShapeDtypeStruct((16, NODE_DEV), wide),
         ),
-        in_specs=[hbm] * 11, out_specs=(hbm, vmem, vmem),
+        in_specs=[hbm] * 11, out_specs=(hbm, vmem),
         scratch_shapes=[
             pltpu.VMEM((6, elem_rows), narrow),
             pltpu.VMEM((elem_rows, nodes), narrow),
@@ -709,6 +733,18 @@
         rve_slot[None, :], slot_element[None, :], jnp.transpose(state_table, (1, 0, 2)),
         loading, compliance,
     )
+    new_table, forces, blocks = pl.pallas_call(
+        deliver_kernel,
+        out_shape=(
+            jax.ShapeDtypeStruct((3, capacity, nodes), wide),
+            jax.ShapeDtypeStruct((3, NODE_DEV), wide),
+            jax.ShapeDtypeStruct((9, NODE_DEV), wide),
+        ),
+        in_specs=[hbm, vmem], out_specs=(hbm, vmem, vmem),
+        scratch_shapes=[pltpu.VMEM((3, capacity, nodes), wide), dma((3, 4)), dma((3, 4))],
+        compiler_params=pltpu.CompilerParams(vmem_limit_bytes=58 * 2**20),
+        name="deliver",
+    )(solved, own_rows)
     return jnp.transpose(new_table, (1, 0, 2)), forces, blocks
 
 

time: 65.4 us -> 65.3 us (level)
  local copies, waits for them, and re-layouts: 4.38 us -> 0 us
  Pallas kernels: 60.2 us -> 64.4 us
    unnamed x7 -> x0, local copies, waits for them, and re-layouts: 4.38 us -> none
    pallas_call x0 -> x1, Pallas kernels: none -> 3.85 us  [tiled_body(): pl.pallas_call(deliver_kernel, out_shape=(jax.ShapeDtypeStruct((3, capaci...]
where the time goes in v5:
time: 65.3 us; the launch traced here: 65.1 us
  Pallas kernels  64.4 us (99%)
    pallas_call x1, Pallas kernels, tiled_body(): pl.pallas_call(step_kernel, out_shape=(jax.ShapeDtypeStruct((3, capacity,...  60.6 us
    pallas_call x1, Pallas kernels, tiled_body(): pl.pallas_call(deliver_kernel, out_shape=(jax.ShapeDtypeStruct((3, capaci...  3.85 us

profile of v5, /device:TPU:0, one launch (start us, length us, event | category | flops | bytes accessed | tf_op | source)
XLA Modules:
  0.0 65.1 jit_solution(13552705199653366070)
XLA Ops:
  0.6 60.6 %step.1 = (f32[3,81,2048]{2,1,0:T(8,128)}, f32[16,128]{1,0:T(8,128)}) custom-call(bf16[6,27]{1,0:T(8,128)(2,1)} %bitcast.8, bf16[27,2048]{1,0:T(8,128)(2,1)} %fiber_hbm.1, f32[12,27]{1,0:T(8,128)} %gradient_hbm.1, f32[1,27]{1,0:T(1,128)} %bitcast.9, s32[4,27]{1,0:T(4,128)} %corner_hbm.1, s32[1,27]{1,0:T(1,128)} %bitcast.10, s32[1,27]{1,0:T(1,128)} %bitcast.11, ...), custom_call_target="tpu_custom_call" | custom-call | tf_op jit(solution)/shard_map/step/pallas_call | solution.py:685
  61.2 3.8 %deliver.1 = (f32[3,81,2048]{2,1,0:T(8,128)}, f32[3,128]{1,0:T(4,128)}, f32[9,128]{1,0:T(8,128)}) custom-call(f32[3,81,2048]{2,1,0:T(8,128)} %get-tuple-element.8.solved_hbm, f32[16,128]{1,0:T(8,128)} %get-tuple-element.9.own_ref), custom_call_target="tpu_custom_call" | custom-call | tf_op jit(solution)/shard_map/deliver/pallas_call | solution.py:736
